TPU v7x, 32 devices: a whole 2x2x4 slice. The times are simulated.
32 devices in a mesh: member: 2 (over y), tile: 4 (over z), face: 4 (over x, core).
Axes of the slice: x: 2, y: 2, z: 4, core: 2. Of those that a mesh axis runs over, the one named last changes fastest.
Arguments:
- atmosphere: float32 [6, 4, 16, 32, 32], P('member', 'face', None, 'tile'), parts along dimension 0, may hold values from -6 to 6
- weight_in: bfloat16 [3, 3, 90, 16], replicated, may hold values from -0.5 to 0.5
- weight_block: bfloat16 [3, 3, 90, 90], replicated, may hold values from -0.21875 to 0.21875
- weight_mix: bfloat16 [90, 90], replicated, may hold values from -0.625 to 0.625
- weight_down: bfloat16 [3, 3, 180, 90], replicated, may hold values from -0.21875 to 0.21875
- weight_coarse: bfloat16 [3, 3, 180, 180], replicated, may hold values from -0.15625 to 0.15625
- weight_decode: bfloat16 [3, 3, 90, 270], replicated, may hold values from -0.125 to 0.125
- readout_matrix: bfloat16 [16, 90], replicated, may hold values from -0.625 to 0.625
Outputs:
- advanced_state: float32 [6, 4, 16, 32, 32], P('member', 'face', None, 'tile'), parts along dimension 0
There are 2 independent parts, one for each index of `member`. A program takes and returns all parts, laid end to end along the dimension named above; an argument that names none is the same for every part. Nothing has to cross between parts.
All inputs are finite; a program needn't handle non-finite values.
Results may differ from a plain program's by a relative error of at most 0.0021.
Values may be sent and summed in bfloat16 or wider, within the bound.
A program may use at most 128 MiB of HBM per device.

v0:
```python
import jax
import jax.numpy as jnp
from jax import lax
from jax.sharding import PartitionSpec as P


def passed_along(block, axis, distance):
    devices = range(lax.axis_size(axis))
    route = [((i - distance) % len(devices), i) for i in devices]
    return lax.ppermute(block, axis, route)


def padded_2(array, sides, width):
    for axis, dim in sides:
        size, length = (lax.axis_size(axis), array.shape[dim])
        up = [(i, (i + 1) % size) for i in range(size)]
        down = [(j, i) for i, j in up]
        last = lax.slice_in_dim(array, length - width, length, axis=dim)
        initial = lax.slice_in_dim(array, 0, width, axis=dim)
        before = lax.ppermute(last, axis, up)
        after = lax.ppermute(initial, axis, down)
        array = jnp.concatenate([before, array, after], axis=dim)
    return array


def zero_corners(rim_rows, halo_width):
    corner = jnp.zeros(rim_rows.shape[:-1] + (halo_width,), rim_rows.dtype)
    return jnp.concatenate([corner, rim_rows[..., halo_width:-halo_width], corner], -1)


def turned_rows(column_block, halo_width):
    corner = jnp.zeros(column_block.shape[:-2] + (halo_width, halo_width), column_block.dtype)
    turned_strip = jnp.flip(jnp.swapaxes(column_block, -1, -2), -2)
    return jnp.concatenate([corner, turned_strip, corner], -1)


def pad_strip(strip_data, halo_width):
    row_count = strip_data.shape[2]
    col_count = strip_data.shape[3]
    tile_count = lax.axis_size("tile")
    tile_pos = lax.axis_index("tile")
    rim_start = col_count - halo_width
    polar_rows = jnp.stack(
        [strip_data[0, :, :halo_width, :], strip_data[2, :, row_count - halo_width :, :]]
    )
    west_cols = jnp.stack([strip_data[0, :, :, rim_start:], strip_data[1, :, :, rim_start:]])
    polar_prev, preceding_sunset_neighbour = passed_along((polar_rows, west_cols), "face", 1)
    east_cols = jnp.stack(
        [
            strip_data[1, :, :, :halo_width],
            strip_data[2, :, :, :halo_width],
            strip_data[0, :, :, :halo_width],
            strip_data[2, :, :, rim_start:],
        ]
    )
    following_sunrise_neighbour = passed_along(east_cols, "face", -1)
    polar_cols = lax.all_gather(following_sunrise_neighbour[2:], "tile", axis=2, tiled=True)
    owner_mask = jnp.stack([tile_pos == 0, tile_pos == tile_count - 1]).reshape(2, 1, 1, 1)
    masked_rows = jnp.where(owner_mask, polar_prev, jnp.zeros_like(polar_prev)).astype(jnp.float32)
    pieces = lax.psum_scatter(
        masked_rows.astype(jnp.bfloat16), "tile", scatter_dimension=3, tiled=True
    )
    left_cols = jnp.stack(
        [
            jnp.flip(jnp.swapaxes(pieces[0], -1, -2), -1),
            preceding_sunset_neighbour[0],
            preceding_sunset_neighbour[1],
        ]
    )
    right_cols = jnp.stack(
        [
            following_sunrise_neighbour[0],
            following_sunrise_neighbour[1],
            jnp.flip(jnp.swapaxes(pieces[1], -1, -2), -1),
        ]
    )
    extended = jnp.concatenate([left_cols, strip_data, right_cols], -1)
    padded = padded_2(extended, (("tile", 2),), halo_width)
    upper_got = padded[:, :, :halo_width, :]
    lower_got = padded[:, :, padded.shape[2] - halo_width :, :]
    upper_face = jnp.stack(
        [
            turned_rows(polar_cols[0], halo_width),
            zero_corners(upper_got[0], halo_width),
            zero_corners(upper_got[1], halo_width),
        ]
    )
    lower_face = jnp.stack(
        [
            zero_corners(lower_got[1], halo_width),
            zero_corners(lower_got[2], halo_width),
            turned_rows(polar_cols[1], halo_width),
        ]
    )
    upper_rows = jnp.where(tile_pos == 0, upper_face, upper_got)
    lower_rows = jnp.where(tile_pos == tile_count - 1, lower_face, lower_got)
    return jnp.concatenate(
        [upper_rows, padded[:, :, halo_width : padded.shape[2] - halo_width, :], lower_rows], 2
    )


def convolve(padded, weight, dilation):
    row_count = padded.shape[2] - 2 * dilation
    col_count = padded.shape[3] - 2 * dilation
    summed = None
    for row_tap in range(3):
        for col_tap in range(3):
            window_patch = padded[
                :,
                :,
                row_tap * dilation : row_tap * dilation + row_count,
                col_tap * dilation : col_tap * dilation + col_count,
            ]
            product = jnp.einsum(
                "oc,fcrn->forn",
                weight[row_tap, col_tap],
                window_patch,
                preferred_element_type=jnp.float32,
            )
            summed = product if summed is None else summed + product
    return summed


def pool_cells(values):
    shape = values.shape
    wide = values.astype(jnp.float32).reshape(shape[:-2] + (shape[-2] // 2, 2, shape[-1] // 2, 2))
    return jnp.mean(wide, axis=(-3, -1))


def upsample(values):
    shape = values.shape
    grown = jnp.broadcast_to(
        values[..., :, None, :, None], shape[:-2] + (shape[-2], 2, shape[-1], 2)
    )
    return grown.reshape(shape[:-2] + (2 * shape[-2], 2 * shape[-1]))


def per_cell_channel_blend(weight, values):
    return jnp.einsum("oc,fcrn->forn", weight, values, preferred_element_type=jnp.float32)


def shards(
    atmosphere,
    weight_in,
    weight_block,
    weight_mix,
    weight_down,
    weight_coarse,
    weight_decode,
    readout_matrix,
):
    variable_grids = atmosphere[:, 0]
    source = variable_grids.astype(jnp.bfloat16)
    encoded = jax.nn.gelu(convolve(pad_strip(source, 1), weight_in, 1)).astype(jnp.bfloat16)
    inner_out = jax.nn.gelu(convolve(pad_strip(encoded, 1), weight_block, 1)).astype(jnp.bfloat16)
    skip_level = (
        encoded.astype(jnp.float32) + per_cell_channel_blend(weight_mix, inner_out)
    ).astype(jnp.bfloat16)
    pooled = pool_cells(skip_level).astype(jnp.bfloat16)
    coarse_one = jax.nn.gelu(convolve(pad_strip(pooled, 2), weight_down, 2)).astype(jnp.bfloat16)
    coarse_two = (
        coarse_one.astype(jnp.float32)
        + jax.nn.gelu(convolve(pad_strip(coarse_one, 1), weight_coarse, 1))
    ).astype(jnp.bfloat16)
    joined_features = jnp.concatenate([upsample(coarse_two), skip_level], 1)
    padded = pad_strip(joined_features, 1)
    upscaled_activations = jax.nn.gelu(convolve(padded, weight_decode, 1)).astype(jnp.bfloat16)
    advanced_state = variable_grids + per_cell_channel_blend(readout_matrix, upscaled_activations)
    return advanced_state[:, None]


def solution(mesh):
    in_specs = (P("member", "face", None, "tile", None), P(), P(), P(), P(), P(), P(), P())
    out_specs = P("member", "face", None, "tile", None)
    return jax.shard_map(shards, mesh=mesh, in_specs=in_specs, out_specs=out_specs, check_vma=False)
```

profile of v0, /device:TPU:0, one launch (start us, length us, event | category | flops | bytes accessed | tf_op | source)
XLA Modules:
  0.0 224.8 jit_solution(17048535610313699755)
XLA Ops:
  6.5 1.0 copy.325
  7.7 0.5 collective-permute-start.1
  8.3 2.7 %collective-permute-start.2 = (bf16[2,16,8,1]{3,1,2,0:T(8,128)(2,1)S(1)}, bf16[2,16,8,1]{3,1,2,0:T(8,128)(2,1)S(1)}, u32[]{:S(2)}, u32[]{:S(2)}) collective-permute-start(bf16[2,16,8,1]{3,1,2,0:T(8,128)(2,1)S(1)} %get-tuple-element.44), channel_id=1, source_target_pairs={{3,0},{0,1},{1,2},{2,3},{7,4},{4,5},{5,6},{6,7},{11,8},{8,9},{9,10... | collective-permute-start | bytes 1544 | tf_op jit(solution)/shard_map/ppermute | solution.py:10
  11.5 0.6 dynamic-slice
  13.8 13.5 %all_gather.15 = bf16[2,16,32,1]{1,0,3,2:T(2,128)(2,1)S(1)} all-gather(bf16[2,16,8,1]{1,0,3,2:T(2,128)(2,1)S(1)} %copy.152), channel_id=1, replica_groups=mesh['member'=2,'tile'=4,'face'=4] {'tile'}, dimensions={2}, use_global_device_ids=true | all-gather | bytes 2560 | tf_op jit(solution)/shard_map/all_gather | solution.py:57
  27.4 18.8 %all-reduce = bf16[2,16,1,32]{1,0,2,3:T(2,128)(2,1)S(1)} all-reduce(bf16[2,16,1,32]{1,0,2,3:T(2,128)(2,1)S(1)} %broadcast_select_fusion.1), channel_id=2, replica_groups=mesh['member'=2,'tile'=4,'face'=4] {'tile'}, use_global_device_ids=true, to_apply=%region_0.1.clone | all-reduce | flops 1024 | bytes 4096
  46.9 2.0 collective-permute-start.3
  48.9 1.5 collective-permute-done.4
  50.5 1.9 collective-permute-done.3
  55.2 0.4 fusion.31
  55.7 1.7 collective-permute-start.6
  57.8 1.1 collective-permute-done.6
  59.1 0.7 reshape.86
  59.9 13.1 %all_gather.16 = bf16[2,90,32,1]{1,3,2,0:T(2,128)(2,1)S(1)} all-gather(bf16[2,90,8,1]{1,3,2,0:T(2,128)(2,1)S(1)} %get-tuple-element.94), channel_id=1, replica_groups=mesh['member'=2,'tile'=4,'face'=4] {'tile'}, dimensions={2}, use_global_device_ids=true | all-gather | bytes 14400 | tf_op jit(solution)/shard_map/all_gather | solution.py:57
  73.0 4.1 %reduce-scatter.7.cloned.1.call-done = bf16[8,180]{1,0:T(8,128)(2,1)} async-done(((bf16[32,180]{1,0:T(8,128)(2,1)}), bf16[8,180]{1,0:T(8,128)(2,1)}) %reduce-scatter.7.cloned.1.call-update) | async-done | bytes 2896
  77.2 0.7 reshape.87
  78.1 0.6 collective-permute-start.9
  78.7 1.6 collective-permute-start.8
  80.2 1.8 collective-permute-done.9
  82.0 2.4 %collective-permute-done.8 = bf16[3,90,1,34]{1,3,2,0:T(8,128)(2,1)S(1)} collective-permute-done((bf16[3,90,1,34]{1,3,2,0:T(8,128)(2,1)S(1)}, bf16[3,90,1,34]{1,3,2,0:T(8,128)(2,1)S(1)}, u32[]{:S(2)}, u32[]{:S(2)}) %collective-permute-start.8) | collective-permute-done | bytes 18392 | tf_op jit(solution)/shard_map/ppermute | solution.py:20
  87.3 1.8 collective-permute-start.10
  89.3 1.1 collective-permute-done.10
  90.5 13.1 %all_gather.17 = bf16[2,90,16,2]{1,3,0,2:T(2,128)(2,1)S(1)} all-gather(bf16[2,90,4,2]{1,3,0,2:T(2,128)(2,1)S(1)} %copy.163), channel_id=1, replica_groups=mesh['member'=2,'tile'=4,'face'=4] {'tile'}, dimensions={2}, use_global_device_ids=true | all-gather | bytes 14400 | tf_op jit(solution)/shard_map/all_gather | solution.py:57
  103.7 15.5 %all-reduce.1 = bf16[2,90,2,16]{1,3,2,0:T(8,128)(2,1)S(1)} all-reduce(bf16[2,90,2,16]{1,3,2,0:T(8,128)(2,1)S(1)} %broadcast_select_fusion.3), channel_id=4, replica_groups=mesh['member'=2,'tile'=4,'face'=4] {'tile'}, use_global_device_ids=true, to_apply=%region_3.4.clone | all-reduce | flops 5760 | bytes 23040
  119.3 1.0 collective-permute-start.14
  120.4 1.2 collective-permute-start.13
  121.5 1.8 collective-permute-done.14
  123.4 2.8 %collective-permute-done.13 = bf16[3,90,2,20]{1,3,2,0:T(8,128)(2,1)S(1)} collective-permute-done((bf16[3,90,2,20]{1,3,2,0:T(8,128)(2,1)S(1)}, bf16[3,90,2,20]{1,3,2,0:T(8,128)(2,1)S(1)}, u32[]{:S(2)}, u32[]{:S(2)}) %collective-permute-start.13) | collective-permute-done | bytes 21632 | tf_op jit(solution)/shard_map/ppermute | solution.py:20
  128.2 1.6 collective-permute-start.16
  130.3 1.2 collective-permute-done.15
  131.6 13.1 %all_gather.18 = bf16[2,180,16,1]{1,3,2,0:T(2,128)(2,1)S(1)} all-gather(bf16[2,180,4,1]{1,3,2,0:T(2,128)(2,1)S(1)} %get-tuple-element.86), channel_id=1, replica_groups=mesh['member'=2,'tile'=4,'face'=4] {'tile'}, dimensions={2}, use_global_device_ids=true | all-gather | bytes 14400 | tf_op jit(solution)/shard_map/all_gather | solution.py:57
  144.8 15.5 %all-reduce.2 = bf16[2,180,1,16]{1,3,2,0:T(8,128)(2,1)S(1)} all-reduce(bf16[2,180,1,16]{1,3,2,0:T(8,128)(2,1)S(1)} %broadcast_select_fusion.2), channel_id=5, replica_groups=mesh['member'=2,'tile'=4,'face'=4] {'tile'}, use_global_device_ids=true, to_apply=%region_4.5.clone | all-reduce | flops 5760 | bytes 23040
  160.4 1.0 collective-permute-start.19
  161.4 1.2 collective-permute-start.18
  162.6 1.8 collective-permute-done.19
  164.4 2.8 %collective-permute-done.18 = bf16[3,180,1,18]{1,3,2,0:T(8,128)(2,1)S(1)} collective-permute-done((bf16[3,180,1,18]{1,3,2,0:T(8,128)(2,1)S(1)}, bf16[3,180,1,18]{1,3,2,0:T(8,128)(2,1)S(1)}, u32[]{:S(2)}, u32[]{:S(2)}) %collective-permute-start.18) | collective-permute-done | bytes 19472 | tf_op jit(solution)/shard_map/ppermute | solution.py:20
  170.3 2.0 collective-permute-start.20
  172.5 1.3 collective-permute-done.20
  173.7 13.1 %all_gather.19 = bf16[2,270,32,1]{1,2,3,0:T(8,128)(2,1)S(1)} all-gather(bf16[2,270,8,1]{1,2,3,0:T(8,128)(2,1)S(1)} %get-tuple-element.84), channel_id=1, replica_groups=mesh['member'=2,'tile'=4,'face'=4] {'tile'}, dimensions={2}, use_global_device_ids=true | all-gather | bytes 43200 | tf_op jit(solution)/shard_map/all_gather | solution.py:57
  187.1 16.2 %all-reduce.3 = bf16[2,270,1,32]{1,3,2,0:T(8,128)(2,1)S(1)} all-reduce(bf16[2,270,1,32]{1,3,2,0:T(8,128)(2,1)S(1)} %copy.172), channel_id=6, replica_groups=mesh['member'=2,'tile'=4,'face'=4] {'tile'}, use_global_device_ids=true, to_apply=%region_5.6.clone | all-reduce | flops 17280 | bytes 69120
  203.4 0.4 fusion.16
  204.0 1.9 collective-permute-start.24
  206.1 2.5 %collective-permute-done.24 = bf16[3,270,1,34]{1,3,2,0:T(8,128)(2,1)S(1)} collective-permute-done((bf16[3,270,1,34]{1,3,2,0:T(8,128)(2,1)S(1)}, bf16[3,270,1,34]{1,3,2,0:T(8,128)(2,1)S(1)}, u32[]{:S(2)}, u32[]{:S(2)}) %collective-permute-start.24) | collective-permute-done | bytes 55112 | tf_op jit(solution)/shard_map/ppermute | solution.py:21
  208.7 3.6 %collective-permute-done.23 = bf16[3,270,1,34]{1,3,2,0:T(8,128)(2,1)S(1)} collective-permute-done((bf16[3,270,1,34]{1,3,2,0:T(8,128)(2,1)S(1)}, bf16[3,270,1,34]{1,3,2,0:T(8,128)(2,1)S(1)}, u32[]{:S(2)}, u32[]{:S(2)}) %collective-permute-start.23) | collective-permute-done | bytes 55112 | tf_op jit(solution)/shard_map/ppermute | solution.py:20
  212.5 0.6 pad_maximum_fusion.1
  213.1 0.5 copy-done.4
  216.6 0.6 fusion.10
  217.2 0.8 copy.179
  (232 shorter events, 18.2 us)
Async XLA Ops:
  6.5 79.7 %copy-start = (bf16[90,90]{1,0:T(8,128)(2,1)S(1)}, bf16[90,90]{1,0:T(8,128)(2,1)}, u32[]{:S(2)}) copy-start(bf16[90,90]{1,0:T(8,128)(2,1)} %param.11) | copy-start | bytes 48604
  6.5 4.6 %copy-start.1 = (f32[3,1,16,8,32]{4,3,2,1,0:T(8,128)S(1)}, f32[3,1,16,8,32]{4,3,2,1,0:T(8,128)}, u32[]{:S(2)}) copy-start(f32[3,1,16,8,32]{4,3,2,1,0:T(8,128)} %param.8) | copy-start | bytes 147460
  6.5 4.7 %copy-start.6 = (bf16[3,3,90,16]{2,3,1,0:T(8,128)(2,1)S(1)}, bf16[3,3,90,16]{2,3,1,0:T(8,128)(2,1)}, u32[]{:S(2)}) copy-start(bf16[3,3,90,16]{2,3,1,0:T(8,128)(2,1)} %param.9) | copy-start | bytes 77764
  6.5 70.6 %reduce-scatter.7.cloned.1.call-start = ((), (), s32[]{:S(2)}) async-start(), calls=%async_computation.1 | async-start | bytes 20480
  7.6 3.9 %copy-start.8 = (u32[32]{0:T(128)S(1)}, u32[32]{0:T(128)}, u32[]{:S(2)}) copy-start(u32[32]{0:T(128)} %constant.6) | copy-start | bytes 388
  7.7 19.6 %collective-permute-start.1 = (bf16[2,16,1,32]{1,0,2,3:T(2,128)(2,1)S(1)}, bf16[2,16,1,32]{1,0,2,3:T(2,128)(2,1)S(1)}, u32[]{:S(2)}, u32[]{:S(2)}) collective-permute-start(bf16[2,16,1,32]{1,0,2,3:T(2,128)(2,1)S(1)} %copy.154), channel_id=1, source_target_pairs={{3,0},{0,1},{1,2},{2,3},{7,4},{4,5},{5,6},{6,7},{11,8},{8,9},{9,10... | collective-permute-start | bytes 6152 | tf_op jit(solution)/shard_map/ppermute | solution.py:10
  8.3 38.2 %collective-permute-start.2 = (bf16[2,16,8,1]{3,1,2,0:T(8,128)(2,1)S(1)}, bf16[2,16,8,1]{3,1,2,0:T(8,128)(2,1)S(1)}, u32[]{:S(2)}, u32[]{:S(2)}) collective-permute-start(bf16[2,16,8,1]{3,1,2,0:T(8,128)(2,1)S(1)} %get-tuple-element.44), channel_id=1, source_target_pairs={{3,0},{0,1},{1,2},{2,3},{7,4},{4,5},{5,6},{6,7},{11,8},{8,9},{9,10... | collective-permute-start | bytes 1544 | tf_op jit(solution)/shard_map/ppermute | solution.py:10
  11.1 2.6 %collective-permute-start = (bf16[4,16,8,1]{3,1,2,0:T(8,128)(2,1)S(1)}, bf16[4,16,8,1]{3,1,2,0:T(8,128)(2,1)S(1)}, u32[]{:S(2)}, u32[]{:S(2)}) collective-permute-start(bf16[4,16,8,1]{3,1,2,0:T(8,128)(2,1)S(1)} %pad_maximum_fusion.14), channel_id=1, source_target_pairs={{1,0},{2,1},{3,2},{0,3},{5,4},{6,5},{7,6},{4,7},{9,8},{10,9},{11,1... | collective-permute-start | bytes 3080 | tf_op jit(solution)/shard_map/ppermute | solution.py:10
  46.6 3.7 %collective-permute-start.4 = (bf16[3,16,1,34]{3,1,2,0:T(8,128)(2,1)S(1)}, bf16[3,16,1,34]{3,1,2,0:T(8,128)(2,1)S(1)}, u32[]{:S(2)}, u32[]{:S(2)}) collective-permute-start(bf16[3,16,1,34]{3,1,2,0:T(8,128)(2,1)S(1)} %get-tuple-element.20), channel_id=1, source_target_pairs={{4,0},{8,4},{12,8},{0,12},{5,1},{9,5},{13,9},{1,13},{6,2},{10,6},{... | collective-permute-start | bytes 9800 | tf_op jit(solution)/shard_map/ppermute | solution.py:21
  46.9 5.5 %collective-permute-start.3 = (bf16[3,16,1,34]{3,1,2,0:T(8,128)(2,1)S(1)}, bf16[3,16,1,34]{3,1,2,0:T(8,128)(2,1)S(1)}, u32[]{:S(2)}, u32[]{:S(2)}) collective-permute-start(bf16[3,16,1,34]{3,1,2,0:T(8,128)(2,1)S(1)} %get-tuple-element.21), channel_id=1, source_target_pairs={{0,4},{4,8},{8,12},{12,0},{1,5},{5,9},{9,13},{13,1},{2,6},{6,10},{... | collective-permute-start | bytes 9800 | tf_op jit(solution)/shard_map/ppermute | solution.py:20
  55.1 2.5 %copy-start.5 = (bf16[3,3,90,90]{3,2,1,0:T(8,128)(2,1)S(1)}, bf16[3,3,90,90]{3,2,1,0:T(8,128)(2,1)}, u32[]{:S(2)}) copy-start(bf16[3,3,90,90]{3,2,1,0:T(8,128)(2,1)} %param.10) | copy-start | bytes 437404
  55.6 22.3 %collective-permute-start.7 = (bf16[2,90,8,1]{1,3,2,0:T(2,128)(2,1)S(1)}, bf16[2,90,8,1]{1,3,2,0:T(2,128)(2,1)S(1)}, u32[]{:S(2)}, u32[]{:S(2)}) collective-permute-start(bf16[2,90,8,1]{1,3,2,0:T(2,128)(2,1)S(1)} %get-tuple-element.26), channel_id=1, source_target_pairs={{3,0},{0,1},{1,2},{2,3},{7,4},{4,5},{5,6},{6,7},{11,8},{8,9},{9,10... | collective-permute-start | bytes 8648 | tf_op jit(solution)/shard_map/ppermute | solution.py:10
  55.7 3.2 %collective-permute-start.6 = (bf16[2,90,1,32]{1,3,2,0:T(8,128)(2,1)S(1)}, bf16[2,90,1,32]{1,3,2,0:T(8,128)(2,1)S(1)}, u32[]{:S(2)}, u32[]{:S(2)}) collective-permute-start(bf16[2,90,1,32]{1,3,2,0:T(8,128)(2,1)S(1)} %pad_maximum_fusion.99), channel_id=1, source_target_pairs={{3,0},{0,1},{1,2},{2,3},{7,4},{4,5},{5,6},{6,7},{11,8},{8,9},{9,10... | collective-permute-start | bytes 34568 | tf_op jit(solution)/shard_map/ppermute | solution.py:10
  57.5 2.4 %collective-permute-start.5 = (bf16[4,90,8,1]{1,3,2,0:T(2,128)(2,1)S(1)}, bf16[4,90,8,1]{1,3,2,0:T(2,128)(2,1)S(1)}, u32[]{:S(2)}, u32[]{:S(2)}) collective-permute-start(bf16[4,90,8,1]{1,3,2,0:T(2,128)(2,1)S(1)} %pad_maximum_fusion.98), channel_id=1, source_target_pairs={{1,0},{2,1},{3,2},{0,3},{5,4},{6,5},{7,6},{4,7},{9,8},{10,9},{11,1... | collective-permute-start | bytes 17288 | tf_op jit(solution)/shard_map/ppermute | solution.py:10
  78.1 3.9 %collective-permute-start.9 = (bf16[3,90,1,34]{1,3,2,0:T(8,128)(2,1)S(1)}, bf16[3,90,1,34]{1,3,2,0:T(8,128)(2,1)S(1)}, u32[]{:S(2)}, u32[]{:S(2)}) collective-permute-start(bf16[3,90,1,34]{1,3,2,0:T(8,128)(2,1)S(1)} %get-tuple-element.24), channel_id=1, source_target_pairs={{4,0},{8,4},{12,8},{0,12},{5,1},{9,5},{13,9},{1,13},{6,2},{10,6},{... | collective-permute-start | bytes 55088 | tf_op jit(solution)/shard_map/ppermute | solution.py:21
  78.7 5.7 %collective-permute-start.8 = (bf16[3,90,1,34]{1,3,2,0:T(8,128)(2,1)S(1)}, bf16[3,90,1,34]{1,3,2,0:T(8,128)(2,1)S(1)}, u32[]{:S(2)}, u32[]{:S(2)}) collective-permute-start(bf16[3,90,1,34]{1,3,2,0:T(8,128)(2,1)S(1)} %get-tuple-element.25), channel_id=1, source_target_pairs={{0,4},{4,8},{8,12},{12,0},{1,5},{5,9},{9,13},{13,1},{2,6},{6,10},{... | collective-permute-start | bytes 55088 | tf_op jit(solution)/shard_map/ppermute | solution.py:20
  86.7 2.4 %copy-start.3 = (bf16[3,3,180,90]{3,2,1,0:T(8,128)(2,1)S(1)}, bf16[3,3,180,90]{3,2,1,0:T(8,128)(2,1)}, u32[]{:S(2)}) copy-start(bf16[3,3,180,90]{3,2,1,0:T(8,128)(2,1)} %param.12) | copy-start | bytes 874804
  87.2 32.1 %collective-permute-start.12 = (bf16[2,90,4,2]{1,3,2,0:T(2,128)(2,1)S(1)}, bf16[2,90,4,2]{1,3,2,0:T(2,128)(2,1)S(1)}, u32[]{:S(2)}, u32[]{:S(2)}) collective-permute-start(bf16[2,90,4,2]{1,3,2,0:T(2,128)(2,1)S(1)} %get-tuple-element.62), channel_id=1, source_target_pairs={{3,0},{0,1},{1,2},{2,3},{7,4},{4,5},{5,6},{6,7},{11,8},{8,9},{9,10... | collective-permute-start | bytes 8648 | tf_op jit(solution)/shard_map/ppermute | solution.py:10
  87.3 3.1 %collective-permute-start.10 = (bf16[4,90,4,2]{1,3,2,0:T(2,128)(2,1)S(1)}, bf16[4,90,4,2]{1,3,2,0:T(2,128)(2,1)S(1)}, u32[]{:S(2)}, u32[]{:S(2)}) collective-permute-start(bf16[4,90,4,2]{1,3,2,0:T(2,128)(2,1)S(1)} %pad_maximum_fusion.119), channel_id=1, source_target_pairs={{1,0},{2,1},{3,2},{0,3},{5,4},{6,5},{7,6},{4,7},{9,8},{10,9},{11,1... | collective-permute-start | bytes 17288 | tf_op jit(solution)/shard_map/ppermute | solution.py:10
  89.3 14.3 %collective-permute-start.11 = (bf16[2,90,2,16]{1,3,2,0:T(8,128)(2,1)S(1)}, bf16[2,90,2,16]{1,3,2,0:T(8,128)(2,1)S(1)}, u32[]{:S(2)}, u32[]{:S(2)}) collective-permute-start(bf16[2,90,2,16]{1,3,2,0:T(8,128)(2,1)S(1)} %pad_maximum_fusion.100), channel_id=1, source_target_pairs={{3,0},{0,1},{1,2},{2,3},{7,4},{4,5},{5,6},{6,7},{11,8},{8,9},{9,10... | collective-permute-start | bytes 34568 | tf_op jit(solution)/shard_map/ppermute | solution.py:10
  119.3 4.0 %collective-permute-start.14 = (bf16[3,90,2,20]{1,3,2,0:T(8,128)(2,1)S(1)}, bf16[3,90,2,20]{1,3,2,0:T(8,128)(2,1)S(1)}, u32[]{:S(2)}, u32[]{:S(2)}) collective-permute-start(bf16[3,90,2,20]{1,3,2,0:T(8,128)(2,1)S(1)} %get-tuple-element.54), channel_id=1, source_target_pairs={{4,0},{8,4},{12,8},{0,12},{5,1},{9,5},{13,9},{1,13},{6,2},{10,6},{... | collective-permute-start | bytes 64808 | tf_op jit(solution)/shard_map/ppermute | solution.py:21
  120.4 5.8 %collective-permute-start.13 = (bf16[3,90,2,20]{1,3,2,0:T(8,128)(2,1)S(1)}, bf16[3,90,2,20]{1,3,2,0:T(8,128)(2,1)S(1)}, u32[]{:S(2)}, u32[]{:S(2)}) collective-permute-start(bf16[3,90,2,20]{1,3,2,0:T(8,128)(2,1)S(1)} %get-tuple-element.55), channel_id=1, source_target_pairs={{0,4},{4,8},{8,12},{12,0},{1,5},{5,9},{9,13},{13,1},{2,6},{6,10},{... | collective-permute-start | bytes 64808 | tf_op jit(solution)/shard_map/ppermute | solution.py:20
  127.4 2.7 %copy-start.2 = (bf16[3,3,180,180]{3,2,1,0:T(8,128)(2,1)S(1)}, bf16[3,3,180,180]{3,2,1,0:T(8,128)(2,1)}, u32[]{:S(2)}) copy-start(bf16[3,3,180,180]{3,2,1,0:T(8,128)(2,1)} %param.13) | copy-start | bytes 1749604
  128.1 32.2 %collective-permute-start.17 = (bf16[2,180,4,1]{1,3,2,0:T(2,128)(2,1)S(1)}, bf16[2,180,4,1]{1,3,2,0:T(2,128)(2,1)S(1)}, u32[]{:S(2)}, u32[]{:S(2)}) collective-permute-start(bf16[2,180,4,1]{1,3,2,0:T(2,128)(2,1)S(1)} %get-tuple-element.38), channel_id=1, source_target_pairs={{3,0},{0,1},{1,2},{2,3},{7,4},{4,5},{5,6},{6,7},{11,8},{8,9},{9,10... | collective-permute-start | bytes 8648 | tf_op jit(solution)/shard_map/ppermute | solution.py:10
  128.2 16.5 %collective-permute-start.16 = (bf16[2,180,1,16]{1,3,2,0:T(8,128)(2,1)S(1)}, bf16[2,180,1,16]{1,3,2,0:T(8,128)(2,1)S(1)}, u32[]{:S(2)}, u32[]{:S(2)}) collective-permute-start(bf16[2,180,1,16]{1,3,2,0:T(8,128)(2,1)S(1)} %pad_maximum_fusion.102), channel_id=1, source_target_pairs={{3,0},{0,1},{1,2},{2,3},{7,4},{4,5},{5,6},{6,7},{11,8},{8,9},{9,10... | collective-permute-start | bytes 34568 | tf_op jit(solution)/shard_map/ppermute | solution.py:10
  129.8 1.7 collective-permute-start.15
  160.4 4.0 %collective-permute-start.19 = (bf16[3,180,1,18]{1,3,2,0:T(8,128)(2,1)S(1)}, bf16[3,180,1,18]{1,3,2,0:T(8,128)(2,1)S(1)}, u32[]{:S(2)}, u32[]{:S(2)}) collective-permute-start(bf16[3,180,1,18]{1,3,2,0:T(8,128)(2,1)S(1)} %get-tuple-element.36), channel_id=1, source_target_pairs={{4,0},{8,4},{12,8},{0,12},{5,1},{9,5},{13,9},{1,13},{6,2},{10,6},{... | collective-permute-start | bytes 58328 | tf_op jit(solution)/shard_map/ppermute | solution.py:21
  161.4 5.8 %collective-permute-start.18 = (bf16[3,180,1,18]{1,3,2,0:T(8,128)(2,1)S(1)}, bf16[3,180,1,18]{1,3,2,0:T(8,128)(2,1)S(1)}, u32[]{:S(2)}, u32[]{:S(2)}) collective-permute-start(bf16[3,180,1,18]{1,3,2,0:T(8,128)(2,1)S(1)} %get-tuple-element.37), channel_id=1, source_target_pairs={{0,4},{4,8},{8,12},{12,0},{1,5},{5,9},{9,13},{13,1},{2,6},{6,10},{... | collective-permute-start | bytes 58328 | tf_op jit(solution)/shard_map/ppermute | solution.py:20
  170.2 33.1 %collective-permute-start.22 = (bf16[2,270,8,1]{1,2,3,0:T(8,128)(2,1)S(1)}, bf16[2,270,8,1]{1,2,3,0:T(8,128)(2,1)S(1)}, u32[]{:S(2)}, u32[]{:S(2)}) collective-permute-start(bf16[2,270,8,1]{1,2,3,0:T(8,128)(2,1)S(1)} %get-tuple-element.12), channel_id=1, source_target_pairs={{3,0},{0,1},{1,2},{2,3},{7,4},{4,5},{5,6},{6,7},{11,8},{8,9},{9,10... | collective-permute-start | bytes 25928 | tf_op jit(solution)/shard_map/ppermute | solution.py:10
  170.3 3.5 %collective-permute-start.20 = (bf16[4,270,8,1]{1,2,3,0:T(8,128)(2,1)S(1)}, bf16[4,270,8,1]{1,2,3,0:T(8,128)(2,1)S(1)}, u32[]{:S(2)}, u32[]{:S(2)}) collective-permute-start(bf16[4,270,8,1]{1,2,3,0:T(8,128)(2,1)S(1)} %pad_maximum_fusion.95), channel_id=1, source_target_pairs={{1,0},{2,1},{3,2},{0,3},{5,4},{6,5},{7,6},{4,7},{9,8},{10,9},{11,1... | collective-permute-start | bytes 51848 | tf_op jit(solution)/shard_map/ppermute | solution.py:10
  172.4 14.5 %collective-permute-start.21 = (bf16[2,270,1,32]{1,2,3,0:T(2,128)(2,1)S(1)}, bf16[2,270,1,32]{1,2,3,0:T(2,128)(2,1)S(1)}, u32[]{:S(2)}, u32[]{:S(2)}) collective-permute-start(bf16[2,270,1,32]{1,2,3,0:T(2,128)(2,1)S(1)} %pad_maximum_fusion.31), channel_id=1, source_target_pairs={{3,0},{0,1},{1,2},{2,3},{7,4},{4,5},{5,6},{6,7},{11,8},{8,9},{9,10... | collective-permute-start | bytes 103688 | tf_op jit(solution)/shard_map/ppermute | solution.py:10
  204.0 4.6 %collective-permute-start.24 = (bf16[3,270,1,34]{1,3,2,0:T(8,128)(2,1)S(1)}, bf16[3,270,1,34]{1,3,2,0:T(8,128)(2,1)S(1)}, u32[]{:S(2)}, u32[]{:S(2)}) collective-permute-start(bf16[3,270,1,34]{1,3,2,0:T(8,128)(2,1)S(1)} %get-tuple-element.7), channel_id=1, source_target_pairs={{4,0},{8,4},{12,8},{0,12},{5,1},{9,5},{13,9},{1,13},{6,2},{10,6},{... | collective-permute-start | bytes 165248 | tf_op jit(solution)/shard_map/ppermute | solution.py:21
  205.9 6.3 %collective-permute-start.23 = (bf16[3,270,1,34]{1,3,2,0:T(8,128)(2,1)S(1)}, bf16[3,270,1,34]{1,3,2,0:T(8,128)(2,1)S(1)}, u32[]{:S(2)}, u32[]{:S(2)}) collective-permute-start(bf16[3,270,1,34]{1,3,2,0:T(8,128)(2,1)S(1)} %get-tuple-element.8), channel_id=1, source_target_pairs={{0,4},{4,8},{8,12},{12,0},{1,5},{5,9},{9,13},{13,1},{2,6},{6,10},{... | collective-permute-start | bytes 165248 | tf_op jit(solution)/shard_map/ppermute | solution.py:20
  212.5 1.1 copy-start.4
  215.9 0.7 copy-start.7
Sparse Core Ops, SparseCore 0:
  60.0 17.1 reduce-scatter.6
where the time goes:
time: 225 us
  blocking collectives  132 us (59%)
  waiting for transfers between devices  32 us (14%)
  starting transfers between devices  21.5 us (10%)
  between operations  15.9 us (7%)
  matrix products  11.8 us (5%)
  local copies, waits for them, and re-layouts  7.52 us (3%)
  other arithmetic  3.83 us (2%)
    all_gather x5, blocking collectives, pad_strip(): lax.all_gather(following_sunrise_neighbour[2:], 'tile', axis=2, tiled=True)  66.1 us
    unnamed x4, blocking collectives  66 us
    ppermute x5, waiting for transfers between devices, padded_2(): before = lax.ppermute(last, axis, up)  13.5 us
    ppermute x15, starting transfers between devices, passed_along(): return lax.ppermute(block, axis, route)  11 us
    dot_general x43, matrix products, convolve(): jnp.einsum('oc,fcrn->forn', weight[row_tap, col_tap], window_patch, prefe...  10.8 us
    ppermute x5, waiting for transfers between devices, padded_2(): after = lax.ppermute(initial, axis, down)  9.37 us
    ppermute x5, starting transfers between devices, padded_2(): before = lax.ppermute(last, axis, up)  6.09 us
    ppermute x15, waiting for transfers between devices, passed_along(): return lax.ppermute(block, axis, route)  5.03 us
  transfers between devices with their start and end apart: 26, of which 16 were waited for; matrix products, arithmetic and copies ran while one was open for 2% of the time, Pallas kernels for 0%

commit v1 on v0

v1 whole, which is shorter than its diff:
```python
import functools

import jax
import jax.numpy as jnp
from jax import lax
from jax.experimental import pallas as pl
from jax.experimental.pallas import tpu as pltpu
from jax.sharding import PartitionSpec as P

LANES = 128
EDGE = 8
F32 = jnp.float32
BF16 = jnp.bfloat16


def groups_of(channels):
    return -(-channels // LANES)


class Halo:
    def __init__(self, refs, rows, cols, width, groups, tiles):
        self.rows, self.cols, self.width = rows, cols, width
        self.groups, self.tiles = groups, tiles
        (self.x, self.sa, self.sb, self.sc, self.sd, self.se, self.sf, self.ra, self.rb,
         self.ru, self.rd, self.pc, self.pd, self.pe, self.pf, self.send, self.recv) = refs

    @staticmethod
    def shapes(rows, cols, width, groups, tiles):
        grid = (groups, 3, rows + 2 * width, cols + 2 * EDGE, LANES)
        pair = (groups, 2, width, rows, LANES)
        single = (groups, width, rows, LANES)
        long = (groups, width, rows + 2 * width, LANES)
        strip = (groups, 3, width, cols, LANES)
        count = 10 + 2 * tiles
        shapes = [grid, pair, pair, single, single, (tiles,) + long, (tiles,) + long,
                  (3,) + pair, (3,) + pair, strip, strip,
                  (tiles,) + single, (tiles,) + single, long, long]
        return [pltpu.VMEM(s, F32) for s in shapes] + [
            pltpu.SemaphoreType.DMA((count,)),
            pltpu.SemaphoreType.DMA((count,)),
        ]

    def copy(self, src, dst, send, recv, tile, face):
        return pltpu.make_async_remote_copy(
            src_ref=src, dst_ref=dst, send_sem=self.send.at[send], recv_sem=self.recv.at[recv],
            device_id={"tile": tile, "face": face}, device_id_type=pl.DeviceIdType.MESH)

    def copies(self, *names):
        tiles, w, rows, cols = self.tiles, self.width, self.rows, self.cols
        t, g = lax.axis_index("tile"), lax.axis_index("face")
        faces = lax.axis_size("face")
        west, east = lax.rem(g + faces - 1, faces), lax.rem(g + 1, faces)
        inner = pl.ds(EDGE, cols)
        found = []
        for name in names:
            if name == "common":
                for step in range(3):
                    to = lax.rem(t + tiles + step - 1, tiles)
                    found.append(self.copy(self.sa, self.ra.at[step], step, step, to, west))
                    found.append(self.copy(self.sb, self.rb.at[step], 3 + step, 3 + step, to, east))
                up, down = lax.rem(t + tiles - 1, tiles), lax.rem(t + 1, tiles)
                found.append(self.copy(self.x.at[:, :, pl.ds(w, w), inner, :], self.rd, 6, 6, up, g))
                found.append(self.copy(self.x.at[:, :, pl.ds(rows, w), inner, :], self.ru, 7, 7, down, g))
            elif name == "to_top":
                found.append(self.copy(self.sc, self.pc.at[t], 8, 10 + t, 0, west))
            elif name == "to_bottom":
                found.append(self.copy(self.sd, self.pd.at[t], 9, 10 + tiles + t, tiles - 1, west))
            for i in range(tiles):
                if name == "from_top":
                    found.append(self.copy(self.se.at[i], self.pe, 10 + i, 8, i, east))
                elif name == "from_bottom":
                    found.append(self.copy(self.sf.at[i], self.pf, 10 + tiles + i, 9, i, east))
                elif name == "at_top":
                    found.append(self.copy(self.sc, self.pc.at[i], 8, 10 + i, 0, west))
                elif name == "at_bottom":
                    found.append(self.copy(self.sd, self.pd.at[i], 9, 10 + tiles + i, 0, west))
        return found

    def start(self):
        tiles, w, rows, cols, x = self.tiles, self.width, self.rows, self.cols, self.x
        t = lax.axis_index("tile")
        for q in range(self.groups):
            for k in range(w):
                own = pl.ds(w, rows)
                first, last = EDGE + k, EDGE + cols - 1 - k
                self.sa[q, 0, k] = x[q, 1, own, first, :]
                self.sa[q, 1, k] = x[q, 2, own, first, :]
                self.sb[q, 0, k] = x[q, 0, own, last, :]
                self.sb[q, 1, k] = x[q, 1, own, last, :]
                self.sc[q, k] = x[q, 0, own, first, :]
                self.sd[q, k] = x[q, 2, own, last, :]
        for c in self.copies("common", "to_top", "to_bottom"):
            c.start()

        @pl.when(t == 0)
        def _():
            for i, c in enumerate(self.copies("from_top")):
                for q in range(self.groups):
                    for k in range(w):
                        self.se[i, q, k] = x[q, 0, w + k, pl.ds(EDGE + i * rows - w, rows + 2 * w), :]
                c.start()

        @pl.when(t == tiles - 1)
        def _():
            for i, c in enumerate(self.copies("from_bottom")):
                for q in range(self.groups):
                    for k in range(w):
                        self.sf[i, q, k] = x[
                            q, 2, w + rows - 1 - k, pl.ds(EDGE + i * rows - w, rows + 2 * w), :]
                c.start()

    def finish(self):
        tiles, w, rows, cols, x = self.tiles, self.width, self.rows, self.cols, self.x
        t = lax.axis_index("tile")
        for c in self.copies("common"):
            c.wait_recv()
        self.copy(self.se.at[0], self.pe, 10, 8, 0, 0).wait_recv()
        self.copy(self.sf.at[0], self.pf, 10, 9, 0, 0).wait_recv()
        for q in range(self.groups):
            for k in range(w):
                left, right = EDGE - 1 - k, EDGE + cols + k
                for f in range(2):
                    for face, col, got in ((1 + f, left, self.rb), (f, right, self.ra)):
                        x[q, face, pl.ds(w, rows), col, :] = got[1, q, f, k]
                        x[q, face, pl.ds(0, w), col, :] = got[2, q, f, k, pl.ds(rows - w, w), :]
                        x[q, face, pl.ds(w + rows, w), col, :] = got[0, q, f, k, pl.ds(0, w), :]
                x[q, 0, :, left, :] = self.pe[q, k]
                x[q, 2, :, right, :] = self.pf[q, k]
        for q in range(self.groups):
            for f in range(3):
                x[q, f, pl.ds(0, w), pl.ds(EDGE, cols), :] = self.ru[q, f]
                x[q, f, pl.ds(w + rows, w), pl.ds(EDGE, cols), :] = self.rd[q, f]
        blank = jnp.zeros((w, EDGE, LANES), F32)

        @pl.when(t == 0)
        def _():
            for c in self.copies("at_top"):
                c.wait_recv()
            for q in range(self.groups):
                for f in range(2):
                    x[q, 1 + f, pl.ds(0, w), pl.ds(EDGE, cols), :] = self.ru[q, f]
                for f in range(3):
                    x[q, f, pl.ds(0, w), pl.ds(0, EDGE), :] = blank
                    x[q, f, pl.ds(0, w), pl.ds(EDGE + cols, EDGE), :] = blank
                for k in range(w):
                    for i in range(tiles):
                        x[q, 0, w - 1 - k, pl.ds(EDGE + i * rows, rows), :] = self.pc[i, q, k]

        @pl.when(t == tiles - 1)
        def _():
            for c in self.copies("at_bottom"):
                c.wait_recv()
            for q in range(self.groups):
                for f in range(2):
                    x[q, f, pl.ds(w + rows, w), pl.ds(EDGE, cols), :] = self.rd[q, 1 + f]
                for f in range(3):
                    x[q, f, pl.ds(w + rows, w), pl.ds(0, EDGE), :] = blank
                    x[q, f, pl.ds(w + rows, w), pl.ds(EDGE + cols, EDGE), :] = blank
                for k in range(w):
                    for i in range(tiles):
                        x[q, 2, w + rows + k, pl.ds(EDGE + i * rows, rows), :] = self.pd[i, q, k]

    def drain(self):
        t = lax.axis_index("tile")
        for c in self.copies("common", "to_top", "to_bottom"):
            c.wait_send()

        @pl.when(t == 0)
        def _():
            for c in self.copies("from_top"):
                c.wait_send()

        @pl.when(t == self.tiles - 1)
        def _():
            for c in self.copies("from_bottom"):
                c.wait_send()


def blocks(rows, cols, body):
    if 3 * rows * cols <= 1024:
        body(0, 3, 0, rows)
        return
    height = max(1, min(rows, 512 // cols))
    per_face = rows // height

    @pl.loop(0, 3 * per_face)
    def _(i):
        body(i // per_face, 1, lax.rem(i, per_face) * height, height)


def conv_block(fields, weights, cols, dilation, face, faces, row, height):
    windows = []
    for tap in range(3):
        for field in fields:
            for q in range(field.shape[0]):
                got = field[q, pl.ds(face, faces), pl.ds(row, height + 2 * dilation),
                            pl.ds(EDGE + dilation * (tap - 1), cols), :]
                windows.append((tap, got.astype(BF16)))
    total = None
    for up in range(3):
        cut = [v[:, up * dilation : up * dilation + height].reshape(faces * height * cols, LANES)
               for _, v in windows]
        lhs = jnp.concatenate(cut, -1)
        rhs = jnp.concatenate([weights[up, tap] for tap in range(3)], -1)
        term = lax.dot_general(lhs, rhs, (((1,), (1,)), ((), ())), preferred_element_type=F32)
        total = term if total is None else total + term
    return total


def rounded(v):
    return v.astype(BF16).astype(F32)


def put(x, value, width, cols, face, faces, row, height):
    for q in range(x.shape[0]):
        part = value[:, q * LANES : (q + 1) * LANES].reshape(faces, height, cols, LANES)
        x[q, pl.ds(face, faces), pl.ds(width + row, height), pl.ds(EDGE, cols), :] = part


def get(x, width, cols, face, faces, row, height):
    parts = [
        x[q, pl.ds(face, faces), pl.ds(width + row, height), pl.ds(EDGE, cols), :].reshape(
            faces * height * cols, LANES)
        for q in range(x.shape[0])
    ]
    return jnp.concatenate(parts, -1) if len(parts) > 1 else parts[0]


def greet(tiles):
    t, g = lax.axis_index("tile"), lax.axis_index("face")
    faces = lax.axis_size("face")
    barrier = pltpu.get_barrier_semaphore()

    def signal(tile, face):
        pl.semaphore_signal(barrier, inc=1, device_id={"tile": tile, "face": face},
                            device_id_type=pl.DeviceIdType.MESH)

    for i in range(tiles):
        signal(i, lax.rem(g + 1, faces))
        signal(i, lax.rem(g + faces - 1, faces))
    signal(lax.rem(t + 1, tiles), g)
    signal(lax.rem(t + tiles - 1, tiles), g)
    pl.semaphore_wait(barrier, 2 * tiles + 2)


def kernel(plans, tiles, src, w_in, w_block, w_mix, w_down, w_coarse, w_decode, w_out, out, *scratch):
    halos = []
    for i, plan in enumerate(plans):
        halos.append(Halo(scratch[17 * i : 17 * i + 17], *plan, tiles))
    wide = scratch[17 * len(plans)]
    source, encoded, skip, pooled, one, two = halos
    rows, cols = source.rows, source.cols
    c_rows, c_cols = pooled.rows, pooled.cols

    def first(*at):
        face, faces, row, height = at
        v = src[pl.ds(face, faces), pl.ds(row, height), :, :]
        source.x[0, pl.ds(face, faces), pl.ds(1 + row, height), pl.ds(EDGE, cols), :] = rounded(v)

    blocks(rows, cols, first)
    greet(tiles)
    source.start()
    source.finish()

    def encode(*at):
        v = rounded(jax.nn.gelu(conv_block([source.x], w_in, cols, 1, *at)))
        put(encoded.x, v, 1, cols, *at)

    blocks(rows, cols, encode)
    encoded.start()
    encoded.finish()

    def block(*at):
        v = jax.nn.gelu(conv_block([encoded.x], w_block, cols, 1, *at)).astype(BF16)
        mixed = lax.dot_general(v, w_mix[...], (((1,), (1,)), ((), ())), preferred_element_type=F32)
        put(skip.x, rounded(get(encoded.x, 1, cols, *at) + mixed), 1, cols, *at)

    blocks(rows, cols, block)

    for f in range(3):
        for r in range(c_rows):
            total = None
            for i in range(2):
                for j in range(2):
                    v = skip.x[0, f, 1 + 2 * r + i, pl.ds(EDGE + j, c_cols, stride=2), :]
                    total = v if total is None else total + v
            pooled.x[0, f, 2 + r, pl.ds(EDGE, c_cols), :] = rounded(total * 0.25)
    pooled.start()
    skip.start()
    pooled.finish()

    def down(*at):
        v = rounded(jax.nn.gelu(conv_block([pooled.x], w_down, c_cols, 2, *at)))
        put(one.x, v, 1, c_cols, *at)

    blocks(c_rows, c_cols, down)
    one.start()
    one.finish()

    def coarse(*at):
        v = jax.nn.gelu(conv_block([one.x], w_coarse, c_cols, 1, *at))
        put(two.x, rounded(get(one.x, 1, c_cols, *at) + v), 1, c_cols, *at)

    blocks(c_rows, c_cols, coarse)
    two.start()
    skip.finish()
    two.finish()

    for q in range(wide.shape[0]):
        for f in range(3):
            for r in range(c_rows + 2):
                targets = [p for p in (2 * r - 1, 2 * r) if 0 <= p < rows + 2]
                v = two.x[q, f, r, pl.ds(EDGE, c_cols), :]
                rim_left = two.x[q, f, r, pl.ds(EDGE - 1, 1), :]
                rim_right = two.x[q, f, r, pl.ds(EDGE + c_cols, 1), :]
                for p in targets:
                    wide[q, f, p, pl.ds(EDGE, c_cols, stride=2), :] = v
                    wide[q, f, p, pl.ds(EDGE + 1, c_cols, stride=2), :] = v
                    wide[q, f, p, pl.ds(EDGE - 1, 1), :] = rim_left
                    wide[q, f, p, pl.ds(EDGE + cols, 1), :] = rim_right

    def decode(*at):
        face, faces, row, height = at
        v = jax.nn.gelu(conv_block([wide, skip.x], w_decode, cols, 1, *at)).astype(BF16)
        read = lax.dot_general(w_out[...], v, (((1,), (1,)), ((), ())), preferred_element_type=F32)
        if faces == 3:
            for f in range(3):
                out[f] = read[:, f * rows * cols : (f + 1) * rows * cols]
        else:
            size = height * cols
            out[face, :, pl.ds(pl.multiple_of(row * cols, size), size)] = read

    blocks(rows, cols, decode)
    for halo in halos:
        halo.drain()


def widened(weight, parts):
    outs = weight.shape[-2]
    sections, at = [], 0
    for size in parts:
        section = weight[..., at : at + size]
        pad = [(0, 0)] * (weight.ndim - 2)
        pad += [(0, groups_of(outs) * LANES - outs), (0, groups_of(size) * LANES - size)]
        sections.append(jnp.pad(section, pad))
        at += size
    return jnp.concatenate(sections, -1) if len(sections) > 1 else sections[0]


def shards(atmosphere, weight_in, weight_block, weight_mix, weight_down, weight_coarse,
           weight_decode, readout_matrix):
    state = atmosphere[:, 0]
    _, fields, rows, cols = state.shape
    tiles = lax.axis_size("tile")
    c0, c1 = weight_block.shape[2], weight_down.shape[2]
    src = jnp.pad(jnp.transpose(state, (0, 2, 3, 1)), [(0, 0)] * 3 + [(0, LANES - fields)])
    g0, g1 = groups_of(c0), groups_of(c1)
    plans = [
        (rows, cols, 1, 1),
        (rows, cols, 1, g0),
        (rows, cols, 1, g0),
        (rows // 2, cols // 2, 2, g0),
        (rows // 2, cols // 2, 1, g1),
        (rows // 2, cols // 2, 1, g1),
    ]
    scratch = [s for plan in plans for s in Halo.shapes(*plan, tiles)]
    scratch.append(pltpu.VMEM((g1, 3, rows + 2, cols + 2 * EDGE, LANES), F32))
    weights = [
        widened(weight_in, (fields,)),
        widened(weight_block, (c0,)),
        widened(weight_mix, (c0,)),
        widened(weight_down, (c0,)),
        widened(weight_coarse, (c1,)),
        widened(weight_decode, (c1, c0)),
        jnp.pad(readout_matrix, [(0, 0), (0, g0 * LANES - c0)]),
    ]
    read = pl.pallas_call(
        functools.partial(kernel, plans, tiles),
        out_shape=jax.ShapeDtypeStruct((3, fields, rows * cols), F32),
        in_specs=[pl.BlockSpec(memory_space=pltpu.VMEM)] * 8,
        out_specs=pl.BlockSpec(memory_space=pltpu.VMEM),
        scratch_shapes=scratch,
        compiler_params=pltpu.CompilerParams(
            collective_id=0, has_side_effects=True, vmem_limit_bytes=60 * 1024 * 1024),
    )(src, *weights)
    return (state + read.reshape(state.shape))[:, None]


def solution(mesh):
    in_specs = (P("member", "face", None, "tile", None), P(), P(), P(), P(), P(), P(), P())
    out_specs = P("member", "face", None, "tile", None)
    return jax.shard_map(shards, mesh=mesh, in_specs=in_specs, out_specs=out_specs, check_vma=False)
```

time: 225 us -> 59.2 us (0.26)
  blocking collectives: 132 us -> 0 us
  Pallas kernels: 0 us -> 46.2 us
  waiting for transfers between devices: 32 us -> 0 us
  starting transfers between devices: 21.5 us -> 0 us
  between operations: 15.9 us -> 0.04 us
  matrix products: 11.8 us -> 0 us
  local copies, waits for them, and re-layouts: 7.52 us -> 10.7 us
    all_gather x5 -> x0, blocking collectives: 66.1 us -> none  [pad_strip(): lax.all_gather(following_sunrise_neighbour[2:], 'tile', axis=2, tiled=True)]
    unnamed x4 -> x0, blocking collectives: 66 us -> none
    pallas_call x0 -> x1, Pallas kernels: none -> 46.2 us  [shards(): pl.pallas_call(functools.partial(kernel, plans, tiles), out_shape=jax.Sha...]
    ppermute x25 -> x0, waiting for transfers between devices: 27.9 us -> none  [the longest x5 13.5 us: padded_2(): before = lax.ppermute(last, axis, up)]
    ppermute x25 -> x0, starting transfers between devices: 21.5 us -> none  [the longest x15 11 us: passed_along(): return lax.ppermute(block, axis, route)]
    dot_general x45 -> x0, matrix products: 11.8 us -> none  [the longest x43 10.8 us: convolve(): jnp.einsum('oc,fcrn->forn', weight[row_tap, col_tap], window_patch, prefe...]
    pad x0 -> x7, local copies, waits for them, and re-layouts: none -> 7.19 us  [the longest x5 5.06 us: widened(): sections.append(jnp.pad(section, pad))]
    unnamed x2 -> x0, waiting for transfers between devices: 4.16 us -> none
  transfers between devices with their start and end apart: 26 -> 0, of which waited for: 16 -> 0; matrix products, arithmetic and copies ran while one was open for 2% -> 0% of each run, Pallas kernels for 0% -> 0%
where the time goes in v1:
time: 59.2 us; the launch traced here: 58.8 us
  Pallas kernels  46.2 us (78%)
  local copies, waits for them, and re-layouts  10.7 us (18%)
  other arithmetic  1.82 us (3%)
    pallas_call x1, Pallas kernels, shards(): pl.pallas_call(functools.partial(kernel, plans, tiles), out_shape=jax.Sha...  46.2 us
    pad x5, local copies, waits for them, and re-layouts, widened(): sections.append(jnp.pad(section, pad))  5.06 us
    unnamed x12, local copies, waits for them, and re-layouts  1.63 us
    pad x1, local copies, waits for them, and re-layouts, shards(): jnp.pad(readout_matrix, [(0, 0), (0, g0 * LANES - c0)])  1.34 us

profile of v1, /device:TPU:0, one launch (start us, length us, event | category | flops | bytes accessed | tf_op | source)
XLA Modules:
  0.0 58.8 jit_solution(6370136085141046051)
XLA Ops:
  0.0 0.0 copy-start.1
  0.0 0.0 copy-start.3
  0.0 1.3 %pad.43.w_out = bf16[16,128]{1,0:T(8,128)(2,1)} pad(bf16[16,90]{1,0:T(8,128)(2,1)} %param.15, bf16[]{:T(256)} %constant.4.clone.1), padding=0_0x0_38 | pad | bytes 6978 | tf_op jit(solution)/shard_map/jit(_pad)/pad | solution.py:375
  1.3 1.4 %pad.38.w_mix = bf16[128,128]{1,0:T(8,128)(2,1)} pad(bf16[90,90]{1,0:T(8,128)(2,1)} %param.11, bf16[]{:T(256)} %constant.4.clone.1), padding=0_38x0_38 | pad | bytes 48970 | tf_op jit(solution)/shard_map/jit(_pad)/pad | solution.py:345
  2.7 0.9 %copy.10 = bf16[3,3,90,16]{3,2,1,0:T(8,128)(2,1)S(1)} copy(bf16[3,3,90,16]{2,3,1,0:T(8,128)(2,1)} %param.9) | data formatting | bytes 51840 | tf_op args[1]
  3.6 0.8 %pad.36.w_in = bf16[3,3,128,128]{3,2,1,0:T(8,128)(2,1)} pad(bf16[3,3,90,16]{3,2,1,0:T(8,128)(2,1)S(1)} %copy.10, bf16[]{:T(256)} %constant.4.clone.1), padding=0_0x0_0x0_38x0_112 | pad | bytes 320834 | tf_op jit(solution)/shard_map/jit(_pad)/pad | solution.py:345
  4.4 1.0 %slice.7 = bf16[3,3,90,90]{2,3,1,0:T(8,128)(2,1)S(1)} slice(bf16[3,3,90,270]{2,3,1,0:T(8,128)(2,1)} %param.14), slice={[0:3], [0:3], [0:90], [180:270]} | slice | bytes 291600 | tf_op jit(solution)/shard_map/slice | solution.py:342
  5.4 0.2 copy.15
  5.6 0.0 copy-done.3
  5.7 0.8 %pad.37.w_block = bf16[3,3,128,128]{3,2,1,0:T(8,128)(2,1)} pad(bf16[3,3,90,90]{3,2,1,0:T(8,128)(2,1)S(1)} %copy-done.3, bf16[]{:T(256)} %constant.4.clone.1), padding=0_0x0_0x0_38x0_38 | pad | bytes 440714 | tf_op jit(solution)/shard_map/jit(_pad)/pad | solution.py:345
  6.4 0.0 copy-done.1
  6.4 0.0 slice-start
  6.4 0.2 copy.9
  6.6 0.8 %pad.35.src = f32[3,8,32,128]{3,2,1,0:T(8,128)} pad(f32[3,8,32,16]{3,2,1,0:T(8,128)S(1)} %bitcast.5, f32[]{:T(128)} %constant.3.clone.1), padding=0_0x0_0x0_0x0_112 | pad | bytes 442372 | tf_op jit(solution)/shard_map/jit(_pad)/pad | solution.py:356
  7.4 0.0 slice-done
  7.5 0.0 copy-start.2
  7.5 0.3 copy.14
  7.7 0.0 copy-start
  7.7 1.1 %fusion.2.w_decode = bf16[3,3,128,384]{3,2,1,0:T(8,128)(2,1)} fusion(bf16[3,3,90,90]{3,2,1,0:T(8,128)(2,1)S(1)} %copy.15, bf16[3,3,90,180]{3,2,1,0:T(8,128)(2,1)S(1)} %copy.14), kind=kLoop, calls=%fused_computation.4 | loop fusion | flops 3538944 | bytes 1322136 | tf_op jit(solution)/shard_map/concatenate | solution.py:347
  8.9 0.0 copy-done.2
  8.9 0.9 %pad.39.w_down = bf16[3,3,256,128]{3,2,1,0:T(8,128)(2,1)} pad(bf16[3,3,180,90]{3,2,1,0:T(8,128)(2,1)S(1)} %copy-done.2, bf16[]{:T(256)} %constant.4.clone.1), padding=0_0x0_0x0_76x0_38 | pad | bytes 881426 | tf_op jit(solution)/shard_map/jit(_pad)/pad | solution.py:345
  9.8 0.0 copy-done
  9.8 1.2 %pad.40.w_coarse = bf16[3,3,256,256]{3,2,1,0:T(8,128)(2,1)} pad(bf16[3,3,180,180]{3,2,1,0:T(8,128)(2,1)S(1)} %copy-done, bf16[]{:T(256)} %constant.4.clone.1), padding=0_0x0_0x0_76x0_76 | pad | bytes 1762850 | tf_op jit(solution)/shard_map/jit(_pad)/pad | solution.py:345
  11.0 46.2 %shard_map.82 = f32[3,16,256]{2,1,0:T(8,128)} custom-call(f32[3,8,32,128]{3,2,1,0:T(8,128)} %pad.35.src, bf16[3,3,128,128]{3,2,1,0:T(8,128)(2,1)} %pad.36.w_in, bf16[3,3,128,128]{3,2,1,0:T(8,128)(2,1)} %pad.37.w_block, bf16[128,128]{1,0:T(8,128)(2,1)} %pad.38.w_mix, bf16[3,3,256,128]{3,2,1,0:T(8,128)(2,1)} %pad.39.w_down, ...), custom_call_target="tpu_custom_call" | custom-call | tf_op jit(solution)/shard_map/pallas_call | solution.py:377
  57.2 0.9 %reshape.4 = f32[3,1,16,8,32]{4,3,2,0,1:T(8,128)S(1)} reshape(f32[3,16,256]{2,1,0:T(8,128)} %shard_map.82) | data formatting | bytes 98304 | tf_op jit(solution)/shard_map/reshape | solution.py:386
  58.1 0.7 %bitcast_add_fusion = f32[3,1,16,8,32]{4,3,2,1,0:T(8,128)} fusion(f32[3,1,16,8,32]{4,3,2,1,0:T(8,128)S(1)} %copy-done.1, f32[3,1,16,8,32]{4,3,2,0,1:T(8,128)S(1)} %reshape.4), kind=kLoop, calls=%fused_computation.5 | loop fusion | flops 12288 | bytes 147456 | tf_op jit(solution)/shard_map/add | solution.py:386
Async XLA Ops:
  0.0 6.4 %copy-start.1 = (f32[3,1,16,8,32]{4,3,2,1,0:T(8,128)S(1)}, f32[3,1,16,8,32]{4,3,2,1,0:T(8,128)}, u32[]{:S(2)}) copy-start(f32[3,1,16,8,32]{4,3,2,1,0:T(8,128)} %param.8) | copy-start | bytes 147460
  0.0 5.6 %copy-start.3 = (bf16[3,3,90,90]{3,2,1,0:T(8,128)(2,1)S(1)}, bf16[3,3,90,90]{3,2,1,0:T(8,128)(2,1)}, u32[]{:S(2)}) copy-start(bf16[3,3,90,90]{3,2,1,0:T(8,128)(2,1)} %param.10) | copy-start | bytes 437404
  6.4 1.0 %slice-start = ((bf16[3,3,90,270]{2,3,1,0:T(8,128)(2,1)}), bf16[3,3,90,180]{2,3,1,0:T(8,128)(2,1)S(1)}, s32[]{:S(2)}) async-start(bf16[3,3,90,270]{2,3,1,0:T(8,128)(2,1)} %param.14), calls=%async_computation | async-start | bytes 847872 | tf_op jit(solution)/shard_map/slice | solution.py:342
  7.5 1.4 %copy-start.2 = (bf16[3,3,180,90]{3,2,1,0:T(8,128)(2,1)S(1)}, bf16[3,3,180,90]{3,2,1,0:T(8,128)(2,1)}, u32[]{:S(2)}) copy-start(bf16[3,3,180,90]{3,2,1,0:T(8,128)(2,1)} %param.12) | copy-start | bytes 874804
  7.7 2.1 %copy-start = (bf16[3,3,180,180]{3,2,1,0:T(8,128)(2,1)S(1)}, bf16[3,3,180,180]{3,2,1,0:T(8,128)(2,1)}, u32[]{:S(2)}) copy-start(bf16[3,3,180,180]{3,2,1,0:T(8,128)(2,1)} %param.13) | copy-start | bytes 1749604

commit v2 on v1

v2 whole, which is shorter than its diff:
```python
import functools

import jax
import jax.numpy as jnp
from jax import lax
from jax.experimental import pallas as pl
from jax.experimental.pallas import tpu as pltpu
from jax.sharding import PartitionSpec as P

LANES = 128
EDGE = 8
TILE = 16
FIELDS = 20
F32 = jnp.float32
BF16 = jnp.bfloat16


def groups_of(channels):
    return -(-channels // LANES)


class Halo:
    def __init__(self, refs, rows, cols, width, groups, tiles):
        self.rows, self.cols, self.width = rows, cols, width
        self.groups, self.tiles = groups, tiles
        (self.x, self.stage, self.sa, self.sb, self.sc, self.sd, self.se, self.sf, self.su, self.sv,
         self.ra, self.rb, self.ru, self.rd, self.pc, self.pd, self.pe, self.pf,
         self.send, self.recv) = refs

    @staticmethod
    def sizes(rows, width, groups):
        counts = (2 * groups * width * rows, groups * width * rows, groups * width * (rows + 2 * width))
        return [-(-n // TILE) * TILE for n in counts]

    @staticmethod
    def shapes(rows, cols, width, groups, tiles):
        pair, single, long = Halo.sizes(rows, width, groups)
        strip = (groups, 3, width, cols, LANES)
        count = 10 + 2 * tiles
        shapes = [(pair,), (pair,), (single,), (single,), (tiles, long), (tiles, long), strip, strip,
                  (3, pair), (3, pair), strip, strip, (tiles, single), (tiles, single), (long,), (long,)]
        shapes = [s if s is strip else s + (LANES,) for s in shapes]
        return [
            pltpu.VMEM((groups, 3, rows + 2 * width, cols + 2 * EDGE, LANES), F32),
            pltpu.VMEM((max(pair, long), LANES), F32),
        ] + [pltpu.VMEM(s, BF16) for s in shapes] + [
            pltpu.SemaphoreType.DMA((count,)),
            pltpu.SemaphoreType.DMA((count,)),
        ]

    def pack(self, target, pieces):
        at = 0
        for piece in pieces:
            self.stage[pl.ds(at, piece.shape[0]), :] = piece
            at += piece.shape[0]
        target[...] = self.stage[pl.ds(0, target.shape[0]), :].astype(BF16)

    def unpack(self, packet):
        self.stage[pl.ds(0, packet.shape[0]), :] = packet[...].astype(F32)

    def copy(self, src, dst, send, recv, tile, face):
        return pltpu.make_async_remote_copy(
            src_ref=src, dst_ref=dst, send_sem=self.send.at[send], recv_sem=self.recv.at[recv],
            device_id={"tile": tile, "face": face}, device_id_type=pl.DeviceIdType.MESH)

    def copies(self, *names):
        tiles = self.tiles
        t, g = lax.axis_index("tile"), lax.axis_index("face")
        faces = lax.axis_size("face")
        west, east = lax.rem(g + faces - 1, faces), lax.rem(g + 1, faces)
        found = []
        for name in names:
            if name == "common":
                for step in range(3):
                    to = lax.rem(t + tiles + step - 1, tiles)
                    found.append(self.copy(self.sa, self.ra.at[step], step, step, to, west))
                    found.append(self.copy(self.sb, self.rb.at[step], 3 + step, 3 + step, to, east))
            elif name == "rows":
                up, down = lax.rem(t + tiles - 1, tiles), lax.rem(t + 1, tiles)
                found.append(self.copy(self.su, self.rd, 6, 6, up, g))
                found.append(self.copy(self.sv, self.ru, 7, 7, down, g))
            elif name == "to_top":
                found.append(self.copy(self.sc, self.pc.at[t], 8, 10 + t, 0, west))
            elif name == "to_bottom":
                found.append(self.copy(self.sd, self.pd.at[t], 9, 10 + tiles + t, tiles - 1, west))
            for i in range(tiles):
                if name == "from_top":
                    found.append(self.copy(self.se.at[i], self.pe, 10 + i, 8, i, east))
                elif name == "from_bottom":
                    found.append(self.copy(self.sf.at[i], self.pf, 10 + tiles + i, 9, i, east))
                elif name == "at_top":
                    found.append(self.copy(self.sc, self.pc.at[i], 8, 10 + i, 0, west))
                elif name == "at_bottom":
                    found.append(self.copy(self.sd, self.pd.at[i], 9, 10 + tiles + i, 0, west))
        return found

    def start(self):
        tiles, w, rows, cols, x = self.tiles, self.width, self.rows, self.cols, self.x
        t = lax.axis_index("tile")
        own = pl.ds(w, rows)
        planes = [(q, k) for q in range(self.groups) for k in range(w)]
        inner = pl.ds(EDGE, cols)
        for q in range(self.groups):
            for f in range(3):
                self.su[q, f] = x[q, f, pl.ds(w, w), inner, :].astype(BF16)
                self.sv[q, f] = x[q, f, pl.ds(rows, w), inner, :].astype(BF16)
        for c in self.copies("rows"):
            c.start()
        first = [[x[q, f, own, EDGE + k, :] for q, k in planes] for f in range(3)]
        last = [[x[q, f, own, EDGE + cols - 1 - k, :] for q, k in planes] for f in range(3)]
        self.pack(self.sc, first[0])
        self.pack(self.sd, last[2])
        for c in self.copies("to_top", "to_bottom"):
            c.start()
        self.pack(self.sa, first[1] + first[2])
        self.pack(self.sb, last[0] + last[1])
        for c in self.copies("common"):
            c.start()

        def long(i, face, row_of):
            cells = pl.ds(EDGE + i * rows - w, rows + 2 * w)
            return [x[q, face, row_of(k), cells, :] for q, k in planes]

        @pl.when(t == 0)
        def _():
            for i, c in enumerate(self.copies("from_top")):
                self.pack(self.se.at[i], long(i, 0, lambda k: w + k))
                c.start()

        @pl.when(t == tiles - 1)
        def _():
            for i, c in enumerate(self.copies("from_bottom")):
                self.pack(self.sf.at[i], long(i, 2, lambda k: w + rows - 1 - k))
                c.start()

    def finish(self):
        tiles, w, rows, cols, x = self.tiles, self.width, self.rows, self.cols, self.x
        t = lax.axis_index("tile")
        for c in self.copies("common", "rows"):
            c.wait_recv()
        self.copy(self.se.at[0], self.pe, 10, 8, 0, 0).wait_recv()
        self.copy(self.sf.at[0], self.pf, 10, 9, 0, 0).wait_recv()
        planes = [(q, k) for q in range(self.groups) for k in range(w)]
        stage = self.stage
        for got, base, sign in ((self.rb, 1, -1), (self.ra, 0, 1)):
            for step in range(3):
                self.unpack(got.at[step])
                for f in range(2):
                    for n, (q, k) in enumerate(planes):
                        col = EDGE - 1 - k if sign < 0 else EDGE + cols + k
                        at = (f * len(planes) + n) * rows
                        if step == 0:
                            x[q, base + f, pl.ds(w + rows, w), col, :] = stage[pl.ds(at, w), :]
                        elif step == 1:
                            x[q, base + f, pl.ds(w, rows), col, :] = stage[pl.ds(at, rows), :]
                        else:
                            x[q, base + f, pl.ds(0, w), col, :] = stage[pl.ds(at + rows - w, w), :]
        for got, face, sign in ((self.pe, 0, -1), (self.pf, 2, 1)):
            self.unpack(got)
            for n, (q, k) in enumerate(planes):
                col = EDGE - 1 - k if sign < 0 else EDGE + cols + k
                x[q, face, :, col, :] = stage[pl.ds(n * (rows + 2 * w), rows + 2 * w), :]
        inner = pl.ds(EDGE, cols)
        for q in range(self.groups):
            for f in range(3):
                x[q, f, pl.ds(0, w), inner, :] = self.ru[q, f].astype(F32)
                x[q, f, pl.ds(w + rows, w), inner, :] = self.rd[q, f].astype(F32)
        blank = jnp.zeros((w, EDGE, LANES), F32)

        def no_corners(q, at):
            for f in range(3):
                x[q, f, pl.ds(at, w), pl.ds(0, EDGE), :] = blank
                x[q, f, pl.ds(at, w), pl.ds(EDGE + cols, EDGE), :] = blank

        def polar(name, packets, face, row_of):
            for i, c in enumerate(self.copies(name)):
                c.wait_recv()
                self.unpack(packets.at[i])
                for n, (q, k) in enumerate(planes):
                    x[q, face, row_of(k), pl.ds(EDGE + i * rows, rows), :] = stage[pl.ds(n * rows, rows), :]

        @pl.when(t == 0)
        def _():
            for q in range(self.groups):
                for f in range(2):
                    x[q, 1 + f, pl.ds(0, w), inner, :] = self.ru[q, f].astype(F32)
                no_corners(q, 0)
            polar("at_top", self.pc, 0, lambda k: w - 1 - k)

        @pl.when(t == tiles - 1)
        def _():
            for q in range(self.groups):
                for f in range(2):
                    x[q, f, pl.ds(w + rows, w), inner, :] = self.rd[q, 1 + f].astype(F32)
                no_corners(q, w + rows)
            polar("at_bottom", self.pd, 2, lambda k: w + rows + k)

    def drain(self):
        t = lax.axis_index("tile")
        for c in self.copies("common", "rows", "to_top", "to_bottom"):
            c.wait_send()

        @pl.when(t == 0)
        def _():
            for c in self.copies("from_top"):
                c.wait_send()

        @pl.when(t == self.tiles - 1)
        def _():
            for c in self.copies("from_bottom"):
                c.wait_send()


def blocks(rows, cols, body):
    if 3 * rows * cols <= 1024:
        body(0, 3, 0, rows)
        return
    height = max(1, min(rows, 512 // cols))
    per_face = rows // height

    @pl.loop(0, 3 * per_face)
    def _(i):
        body(i // per_face, 1, lax.rem(i, per_face) * height, height)


def conv_block(fields, weights, cols, dilation, face, faces, row, height):
    windows = []
    for tap in range(3):
        for field in fields:
            for q in range(field.shape[0]):
                got = field[q, pl.ds(face, faces), pl.ds(row, height + 2 * dilation),
                            pl.ds(EDGE + dilation * (tap - 1), cols), :]
                windows.append((tap, got.astype(BF16)))
    total = None
    for up in range(3):
        cut = [v[:, up * dilation : up * dilation + height].reshape(faces * height * cols, LANES)
               for _, v in windows]
        lhs = jnp.concatenate(cut, -1)
        term = lax.dot_general(lhs, weights[up], (((1,), (1,)), ((), ())), preferred_element_type=F32)
        total = term if total is None else total + term
    return total


def rounded(v):
    return v.astype(BF16).astype(F32)


def put(x, value, width, cols, face, faces, row, height):
    for q in range(x.shape[0]):
        part = value[:, q * LANES : (q + 1) * LANES].reshape(faces, height, cols, LANES)
        x[q, pl.ds(face, faces), pl.ds(width + row, height), pl.ds(EDGE, cols), :] = part


def get(x, width, cols, face, faces, row, height):
    parts = [
        x[q, pl.ds(face, faces), pl.ds(width + row, height), pl.ds(EDGE, cols), :].reshape(
            faces * height * cols, LANES)
        for q in range(x.shape[0])
    ]
    return jnp.concatenate(parts, -1) if len(parts) > 1 else parts[0]


def greet_first(tiles):
    t, g = lax.axis_index("tile"), lax.axis_index("face")
    faces = lax.axis_size("face")
    barrier = pltpu.get_barrier_semaphore()

    def signal(tile, face):
        pl.semaphore_signal(barrier, inc=1, device_id={"tile": tile, "face": face},
                            device_id_type=pl.DeviceIdType.MESH)

    for i in range(tiles):
        signal(i, lax.rem(g + 1, faces))
        signal(i, lax.rem(g + faces - 1, faces))
    signal(lax.rem(t + 1, tiles), g)
    signal(lax.rem(t + tiles - 1, tiles), g)


def greet_wait(tiles):
    pl.semaphore_wait(pltpu.get_barrier_semaphore(), 2 * tiles + 2)


def widen(wide, weight, parts):
    outs = weight.shape[2]
    step = sum(groups_of(size) for size in parts) * LANES
    wide[...] = jnp.zeros_like(wide)
    for up in range(3):
        for tap in range(3):
            at, begin = tap * step, 0
            for size in parts:
                wide[up, pl.ds(0, outs), pl.ds(at, size)] = weight[up, tap, :, begin : begin + size]
                at += groups_of(size) * LANES
                begin += size


def kernel(plans, tiles, src, w_in, w_block, w_mix, w_down, w_coarse, w_decode, w_out, out, *scratch):
    halos = []
    for i, plan in enumerate(plans):
        halos.append(Halo(scratch[FIELDS * i : FIELDS * i + FIELDS], *plan, tiles))
    wide, k_in, k_block, k_mix, k_down, k_coarse, k_decode, k_out = scratch[FIELDS * len(plans) :]
    source, encoded, skip, pooled, one, two = halos
    rows, cols = source.rows, source.cols
    c_rows, c_cols = pooled.rows, pooled.cols

    greet_first(tiles)

    def first(*at):
        face, faces, row, height = at
        v = rounded(src[pl.ds(face, faces), pl.ds(row, height), :, :])
        place = (0, pl.ds(face, faces), pl.ds(1 + row, height), pl.ds(EDGE, cols))
        source.x[place] = jnp.zeros((faces, height, cols, LANES), F32)
        source.x[place + (pl.ds(0, src.shape[3]),)] = v

    blocks(rows, cols, first)
    greet_wait(tiles)
    source.start()
    fields, c0, c1 = w_in.shape[3], w_block.shape[3], w_coarse.shape[3]
    widen(k_in, w_in, (fields,))
    widen(k_block, w_block, (c0,))
    k_mix[...] = jnp.zeros_like(k_mix)
    k_mix[pl.ds(0, c0), pl.ds(0, c0)] = w_mix[...]
    k_out[...] = jnp.zeros_like(k_out)
    k_out[:, pl.ds(0, c0)] = w_out[...]
    source.finish()

    def encode(*at):
        v = rounded(jax.nn.gelu(conv_block([source.x], k_in, cols, 1, *at)))
        put(encoded.x, v, 1, cols, *at)

    blocks(rows, cols, encode)
    encoded.start()
    widen(k_down, w_down, (c0,))
    widen(k_coarse, w_coarse, (c1,))
    widen(k_decode, w_decode, (c1, c0))
    encoded.finish()

    def block(*at):
        v = jax.nn.gelu(conv_block([encoded.x], k_block, cols, 1, *at)).astype(BF16)
        mixed = lax.dot_general(v, k_mix[...], (((1,), (1,)), ((), ())), preferred_element_type=F32)
        put(skip.x, rounded(get(encoded.x, 1, cols, *at) + mixed), 1, cols, *at)

    blocks(rows, cols, block)

    for f in range(3):
        for r in range(c_rows):
            total = None
            for i in range(2):
                for j in range(2):
                    v = skip.x[0, f, 1 + 2 * r + i, pl.ds(EDGE + j, c_cols, stride=2), :]
                    total = v if total is None else total + v
            pooled.x[0, f, 2 + r, pl.ds(EDGE, c_cols), :] = rounded(total * 0.25)
    pooled.start()
    skip.start()
    pooled.finish()

    def down(*at):
        v = rounded(jax.nn.gelu(conv_block([pooled.x], k_down, c_cols, 2, *at)))
        put(one.x, v, 1, c_cols, *at)

    blocks(c_rows, c_cols, down)
    one.start()
    one.finish()

    def coarse(*at):
        v = jax.nn.gelu(conv_block([one.x], k_coarse, c_cols, 1, *at))
        put(two.x, rounded(get(one.x, 1, c_cols, *at) + v), 1, c_cols, *at)

    blocks(c_rows, c_cols, coarse)
    two.start()
    skip.finish()
    two.finish()

    for q in range(wide.shape[0]):
        for f in range(3):
            for r in range(c_rows + 2):
                targets = [p for p in (2 * r - 1, 2 * r) if 0 <= p < rows + 2]
                v = two.x[q, f, r, pl.ds(EDGE, c_cols), :]
                rim_left = two.x[q, f, r, pl.ds(EDGE - 1, 1), :]
                rim_right = two.x[q, f, r, pl.ds(EDGE + c_cols, 1), :]
                for p in targets:
                    wide[q, f, p, pl.ds(EDGE, c_cols, stride=2), :] = v
                    wide[q, f, p, pl.ds(EDGE + 1, c_cols, stride=2), :] = v
                    wide[q, f, p, pl.ds(EDGE - 1, 1), :] = rim_left
                    wide[q, f, p, pl.ds(EDGE + cols, 1), :] = rim_right

    def decode(*at):
        face, faces, row, height = at
        v = jax.nn.gelu(conv_block([wide, skip.x], k_decode, cols, 1, *at)).astype(BF16)
        read = lax.dot_general(k_out[...], v, (((1,), (1,)), ((), ())), preferred_element_type=F32)
        if faces == 3:
            for f in range(3):
                out[f] = read[:, f * rows * cols : (f + 1) * rows * cols]
        else:
            size = height * cols
            out[face, :, pl.ds(pl.multiple_of(row * cols, size), size)] = read

    blocks(rows, cols, decode)
    for halo in halos:
        halo.drain()


def shards(atmosphere, weight_in, weight_block, weight_mix, weight_down, weight_coarse,
           weight_decode, readout_matrix):
    state = atmosphere[:, 0]
    _, fields, rows, cols = state.shape
    tiles = lax.axis_size("tile")
    c0, c1 = weight_block.shape[2], weight_down.shape[2]
    src = jnp.transpose(state, (0, 2, 3, 1))
    g0, g1 = groups_of(c0), groups_of(c1)
    plans = [
        (rows, cols, 1, 1),
        (rows, cols, 1, g0),
        (rows, cols, 1, g0),
        (rows // 2, cols // 2, 2, g0),
        (rows // 2, cols // 2, 1, g1),
        (rows // 2, cols // 2, 1, g1),
    ]
    scratch = [s for plan in plans for s in Halo.shapes(*plan, tiles)]
    scratch.append(pltpu.VMEM((g1, 3, rows + 2, cols + 2 * EDGE, LANES), F32))
    scratch += [
        pltpu.VMEM(s, BF16)
        for s in (
            (3, g0 * LANES, 3 * LANES),
            (3, g0 * LANES, 3 * g0 * LANES),
            (g0 * LANES, g0 * LANES),
            (3, g1 * LANES, 3 * g0 * LANES),
            (3, g1 * LANES, 3 * g1 * LANES),
            (3, g0 * LANES, 3 * (g1 + g0) * LANES),
            (fields, g0 * LANES),
        )
    ]
    weights = [weight_in, weight_block, weight_mix, weight_down, weight_coarse, weight_decode,
               readout_matrix]
    read = pl.pallas_call(
        functools.partial(kernel, plans, tiles),
        out_shape=jax.ShapeDtypeStruct((3, fields, rows * cols), F32),
        in_specs=[pl.BlockSpec(memory_space=pltpu.VMEM)] * 8,
        out_specs=pl.BlockSpec(memory_space=pltpu.VMEM),
        scratch_shapes=scratch,
        compiler_params=pltpu.CompilerParams(
            collective_id=0, has_side_effects=True, vmem_limit_bytes=60 * 1024 * 1024),
    )(src, *weights)
    return (state + read.reshape(state.shape))[:, None]


def solution(mesh):
    in_specs = (P("member", "face", None, "tile", None), P(), P(), P(), P(), P(), P(), P())
    out_specs = P("member", "face", None, "tile", None)
    return jax.shard_map(shards, mesh=mesh, in_specs=in_specs, out_specs=out_specs, check_vma=False)
```

time: 59.2 us -> 43.8 us (0.74)
  Pallas kernels: 46.2 us -> 38.1 us
  local copies, waits for them, and re-layouts: 10.7 us -> 4.76 us
  other arithmetic: 1.82 us -> 0.7 us
    pallas_call x1, Pallas kernels: 46.2 us -> 38.1 us  [shards(): pl.pallas_call(functools.partial(kernel, plans, tiles), out_shape=jax.Sha...]
    pad x7 -> x0, local copies, waits for them, and re-layouts: 7.19 us -> none  [the longest x5 5.06 us: widened(): sections.append(jnp.pad(section, pad))]
    unnamed x12 -> x7, local copies, waits for them, and re-layouts: 1.63 us -> 3.86 us
    concatenate x1 -> x0, other arithmetic: 1.11 us -> none  [widened(): return jnp.concatenate(sections, -1) if len(sections) > 1 else sections[0]]
    slice x3 -> x0, local copies, waits for them, and re-layouts: 1.02 us -> none  [widened(): section = weight[..., at:at + size]]
where the time goes in v2:
time: 43.8 us; the launch traced here: 43.6 us
  Pallas kernels  38.1 us (87%)
  local copies, waits for them, and re-layouts  4.76 us (11%)
  other arithmetic  0.7 us (2%)
    pallas_call x1, Pallas kernels, shards(): pl.pallas_call(functools.partial(kernel, plans, tiles), out_shape=jax.Sha...  38.1 us
    unnamed x7, local copies, waits for them, and re-layouts  3.86 us
    reshape x1, local copies, waits for them, and re-layouts, shards(): return (state + read.reshape(state.shape))[:, None]  0.9 us

profile of v2, /device:TPU:0, one launch (start us, length us, event | category | flops | bytes accessed | tf_op | source)
XLA Modules:
  0.0 43.6 jit_solution(1382452538318890771)
XLA Ops:
  0.0 0.0 copy-start
  0.0 0.0 copy-start.1
  0.0 1.7 %copy.10.w_in = bf16[3,3,90,16]{3,2,1,0:T(8,128)(2,1)} copy(bf16[3,3,90,16]{2,3,1,0:T(8,128)(2,1)} %param.9) | data formatting | bytes 51840 | tf_op args[1]
  1.7 0.0 copy-done
  1.7 0.9 %copy.9 = f32[3,1,16,8,32]{2,4,3,0,1:T(8,128)} copy(f32[3,1,16,8,32]{4,3,2,1,0:T(8,128)S(1)} %copy-done) | data formatting | bytes 98304 | tf_op args[0]
  2.6 0.0 copy-done.1
  2.7 1.2 %copy.11.w_decode = bf16[3,3,90,270]{3,2,1,0:T(8,128)(2,1)} copy(bf16[3,3,90,270]{2,3,1,0:T(8,128)(2,1)S(1)} %copy-done.1) | data formatting | bytes 874800 | tf_op args[6]
  3.9 38.1 %shard_map.82 = f32[3,16,256]{2,1,0:T(8,128)} custom-call(f32[3,8,32,16]{3,2,1,0:T(8,128)} %bitcast.5, bf16[3,3,90,16]{3,2,1,0:T(8,128)(2,1)} %copy.10.w_in, bf16[3,3,90,90]{3,2,1,0:T(8,128)(2,1)} %w_block.1, bf16[90,90]{1,0:T(8,128)(2,1)} %w_mix.1, bf16[3,3,180,90]{3,2,1,0:T(8,128)(2,1)} %w_down.1, bf16[3,3,180,180]{3,2,1,0:T(8,128)(2,1)} %w_coarse.1, ...), custom_call_target="tpu_custom_call" | custom-call | tf_op jit(solution)/shard_map/pallas_call | solution.py:434
  42.0 0.9 %reshape.4 = f32[3,1,16,8,32]{4,3,2,0,1:T(8,128)S(1)} reshape(f32[3,16,256]{2,1,0:T(8,128)} %shard_map.82) | data formatting | bytes 98304 | tf_op jit(solution)/shard_map/reshape | solution.py:443
  42.9 0.7 %bitcast_add_fusion = f32[3,1,16,8,32]{4,3,2,1,0:T(8,128)} fusion(f32[3,1,16,8,32]{4,3,2,1,0:T(8,128)S(1)} %copy-done, f32[3,1,16,8,32]{4,3,2,0,1:T(8,128)S(1)} %reshape.4), kind=kLoop, calls=%fused_computation | loop fusion | flops 12288 | bytes 147456 | tf_op jit(solution)/shard_map/add | solution.py:443
Async XLA Ops:
  0.0 1.7 %copy-start = (f32[3,1,16,8,32]{4,3,2,1,0:T(8,128)S(1)}, f32[3,1,16,8,32]{4,3,2,1,0:T(8,128)}, u32[]{:S(2)}) copy-start(f32[3,1,16,8,32]{4,3,2,1,0:T(8,128)} %param.8) | copy-start | bytes 147460
  0.0 2.6 %copy-start.1 = (bf16[3,3,90,270]{2,3,1,0:T(8,128)(2,1)S(1)}, bf16[3,3,90,270]{2,3,1,0:T(8,128)(2,1)}, u32[]{:S(2)}) copy-start(bf16[3,3,90,270]{2,3,1,0:T(8,128)(2,1)} %param.14) | copy-start | bytes 1312204

commit v3 on v2

--- a/solution.py
+++ b/solution.py
@@ -236,7 +236,9 @@
         cut = [v[:, up * dilation : up * dilation + height].reshape(faces * height * cols, LANES)
                for _, v in windows]
         lhs = jnp.concatenate(cut, -1)
-        term = lax.dot_general(lhs, weights[up], (((1,), (1,)), ((), ())), preferred_element_type=F32)
+        rhs = weights[up]
+        across = 0 if rhs.shape[0] == lhs.shape[1] else 1
+        term = lax.dot_general(lhs, rhs, (((1,), (across,)), ((), ())), preferred_element_type=F32)
         total = term if total is None else total + term
     return total
 
@@ -278,6 +280,19 @@
 
 def greet_wait(tiles):
     pl.semaphore_wait(pltpu.get_barrier_semaphore(), 2 * tiles + 2)
+
+
+def heighten(tall, weight, parts):
+    outs = weight.shape[3]
+    step = sum(groups_of(size) for size in parts) * LANES
+    tall[...] = jnp.zeros_like(tall)
+    for up in range(3):
+        for tap in range(3):
+            at, begin = tap * step, 0
+            for size in parts:
+                tall[up, pl.ds(at, size), pl.ds(0, outs)] = weight[up, tap, begin : begin + size, :]
+                at += groups_of(size) * LANES
+                begin += size
 
 
 def widen(wide, weight, parts):
@@ -293,7 +308,7 @@
                 begin += size
 
 
-def kernel(plans, tiles, src, w_in, w_block, w_mix, w_down, w_coarse, w_decode, w_out, out, *scratch):
+def kernel(plans, tiles, state, src, w_in, w_block, w_mix, w_down, w_coarse, w_decode, w_out, out, *scratch):
     halos = []
     for i, plan in enumerate(plans):
         halos.append(Halo(scratch[FIELDS * i : FIELDS * i + FIELDS], *plan, tiles))
@@ -314,8 +329,8 @@
     blocks(rows, cols, first)
     greet_wait(tiles)
     source.start()
-    fields, c0, c1 = w_in.shape[3], w_block.shape[3], w_coarse.shape[3]
-    widen(k_in, w_in, (fields,))
+    fields, c0, c1 = w_in.shape[2], w_block.shape[3], w_coarse.shape[3]
+    heighten(k_in, w_in, (fields,))
     widen(k_block, w_block, (c0,))
     k_mix[...] = jnp.zeros_like(k_mix)
     k_mix[pl.ds(0, c0), pl.ds(0, c0)] = w_mix[...]
@@ -331,7 +346,7 @@
     encoded.start()
     widen(k_down, w_down, (c0,))
     widen(k_coarse, w_coarse, (c1,))
-    widen(k_decode, w_decode, (c1, c0))
+    heighten(k_decode, w_decode, (c1, c0))
     encoded.finish()
 
     def block(*at):
@@ -387,12 +402,10 @@
         face, faces, row, height = at
         v = jax.nn.gelu(conv_block([wide, skip.x], k_decode, cols, 1, *at)).astype(BF16)
         read = lax.dot_general(k_out[...], v, (((1,), (1,)), ((), ())), preferred_element_type=F32)
-        if faces == 3:
-            for f in range(3):
-                out[f] = read[:, f * rows * cols : (f + 1) * rows * cols]
-        else:
-            size = height * cols
-            out[face, :, pl.ds(pl.multiple_of(row * cols, size), size)] = read
+        for f in range(faces):
+            for r in range(height):
+                at = (f * height + r) * cols
+                out[face + f, :, row + r, :] = state[face + f, :, row + r, :] + read[:, at : at + cols]
 
     blocks(rows, cols, decode)
     for halo in halos:
@@ -420,27 +433,27 @@
     scratch += [
         pltpu.VMEM(s, BF16)
         for s in (
-            (3, g0 * LANES, 3 * LANES),
+            (3, 3 * LANES, g0 * LANES),
             (3, g0 * LANES, 3 * g0 * LANES),
             (g0 * LANES, g0 * LANES),
             (3, g1 * LANES, 3 * g0 * LANES),
             (3, g1 * LANES, 3 * g1 * LANES),
-            (3, g0 * LANES, 3 * (g1 + g0) * LANES),
+            (3, 3 * (g1 + g0) * LANES, g0 * LANES),
             (fields, g0 * LANES),
         )
     ]
-    weights = [weight_in, weight_block, weight_mix, weight_down, weight_coarse, weight_decode,
-               readout_matrix]
-    read = pl.pallas_call(
+    weights = [jnp.swapaxes(weight_in, 2, 3), weight_block, weight_mix, weight_down, weight_coarse,
+               jnp.swapaxes(weight_decode, 2, 3), readout_matrix]
+    advanced = pl.pallas_call(
         functools.partial(kernel, plans, tiles),
-        out_shape=jax.ShapeDtypeStruct((3, fields, rows * cols), F32),
-        in_specs=[pl.BlockSpec(memory_space=pltpu.VMEM)] * 8,
+        out_shape=jax.ShapeDtypeStruct((3, fields, rows, cols), F32),
+        in_specs=[pl.BlockSpec(memory_space=pltpu.VMEM)] * 9,
         out_specs=pl.BlockSpec(memory_space=pltpu.VMEM),
         scratch_shapes=scratch,
         compiler_params=pltpu.CompilerParams(
             collective_id=0, has_side_effects=True, vmem_limit_bytes=60 * 1024 * 1024),
-    )(src, *weights)
-    return (state + read.reshape(state.shape))[:, None]
+    )(state, src, *weights)
+    return advanced[:, None]
 
 
 def solution(mesh):

time: 43.8 us -> 42 us (0.959)
  local copies, waits for them, and re-layouts: 4.76 us -> 3.47 us
  other arithmetic: 0.7 us -> 0 us
    reshape x1 -> x0, local copies, waits for them, and re-layouts: 0.9 us -> none  [shards(): return (state + read.reshape(state.shape))[:, None]]
    add x1 -> x0, other arithmetic: 0.7 us -> none  [shards(): return (state + read.reshape(state.shape))[:, None]]
    unnamed x7 -> x2, local copies, waits for them, and re-layouts: 3.86 us -> 3.47 us
where the time goes in v3:
time: 42 us; the launch traced here: 41.8 us
  Pallas kernels  38.3 us (91%)
  local copies, waits for them, and re-layouts  3.47 us (8%)
    pallas_call x1, Pallas kernels, shards(): pl.pallas_call(functools.partial(kernel, plans, tiles), out_shape=jax.Sha...  38.3 us
    unnamed x2, local copies, waits for them, and re-layouts  3.47 us

profile of v3, /device:TPU:0, one launch (start us, length us, event | category | flops | bytes accessed | tf_op | source)
XLA Modules:
  0.0 41.8 jit_solution(14081243000435190509)
XLA Ops:
  0.0 1.8 %copy.9 = f32[3,1,16,8,32]{2,4,3,0,1:T(8,128)} copy(f32[3,1,16,8,32]{4,3,2,1,0:T(8,128)} %param.8) | data formatting | bytes 98304 | tf_op args[0]
  1.9 38.3 %shard_map.82 = f32[3,16,8,32]{3,2,1,0:T(8,128)} custom-call(f32[3,16,8,32]{3,2,1,0:T(8,128)} %bitcast.11, f32[3,8,32,16]{3,2,1,0:T(8,128)} %bitcast.9, bf16[3,3,16,90]{3,2,1,0:T(8,128)(2,1)} %bitcast.13, bf16[3,3,90,90]{3,2,1,0:T(8,128)(2,1)} %w_block.1, bf16[90,90]{1,0:T(8,128)(2,1)} %w_mix.1, bf16[3,3,180,90]{3,2,1,0:T(8,128)(2,1)} %w_down.1, ...), custom_call_target="tpu_custom_call" | custom-call | tf_op jit(solution)/shard_map/pallas_call | solution.py:447
  40.2 1.6 %copy.14 = f32[3,1,16,8,32]{4,3,2,1,0:T(8,128)} copy(f32[3,1,16,8,32]{4,3,2,1,0:T(8,128)} %bitcast.10) | data formatting | bytes 98304

commit v4 on v3

--- a/solution.py
+++ b/solution.py
@@ -282,17 +282,13 @@
     pl.semaphore_wait(pltpu.get_barrier_semaphore(), 2 * tiles + 2)
 
 
-def heighten(tall, weight, parts):
+def heighten(tall, weight, begin, size):
     outs = weight.shape[3]
-    step = sum(groups_of(size) for size in parts) * LANES
+    step = groups_of(size) * LANES
     tall[...] = jnp.zeros_like(tall)
     for up in range(3):
         for tap in range(3):
-            at, begin = tap * step, 0
-            for size in parts:
-                tall[up, pl.ds(at, size), pl.ds(0, outs)] = weight[up, tap, begin : begin + size, :]
-                at += groups_of(size) * LANES
-                begin += size
+            tall[up, pl.ds(tap * step, size), pl.ds(0, outs)] = weight[up, tap, begin : begin + size, :]
 
 
 def widen(wide, weight, parts):
@@ -308,29 +304,40 @@
                 begin += size
 
 
-def kernel(plans, tiles, state, src, w_in, w_block, w_mix, w_down, w_coarse, w_decode, w_out, out, *scratch):
+def kernel(plans, tiles, state, *refs):
+    far, (out, *scratch) = refs[:7], refs[7:]
+    near, fetched = scratch[-8:-1], scratch[-1]
+    scratch = scratch[:-8]
+    fetches = [pltpu.make_async_copy(far[i], near[i], fetched.at[i]) for i in range(7)]
+    w_in, w_block, w_mix, w_down, w_coarse, w_decode, w_out = near
     halos = []
     for i, plan in enumerate(plans):
         halos.append(Halo(scratch[FIELDS * i : FIELDS * i + FIELDS], *plan, tiles))
-    wide, k_in, k_block, k_mix, k_down, k_coarse, k_decode, k_out = scratch[FIELDS * len(plans) :]
+    wide, partial, k_in, k_block, k_mix, k_down, k_coarse, k_wide, k_skip, k_out = scratch[FIELDS * len(plans) :]
     source, encoded, skip, pooled, one, two = halos
     rows, cols = source.rows, source.cols
     c_rows, c_cols = pooled.rows, pooled.cols
 
     greet_first(tiles)
+    for fetch in fetches:
+        fetch.start()
 
     def first(*at):
         face, faces, row, height = at
-        v = rounded(src[pl.ds(face, faces), pl.ds(row, height), :, :])
         place = (0, pl.ds(face, faces), pl.ds(1 + row, height), pl.ds(EDGE, cols))
         source.x[place] = jnp.zeros((faces, height, cols, LANES), F32)
-        source.x[place + (pl.ds(0, src.shape[3]),)] = v
+        for f in range(faces):
+            for r in range(height):
+                v = rounded(state[face + f, :, row + r, :]).T
+                source.x[0, face + f, 1 + row + r, pl.ds(EDGE, cols), pl.ds(0, state.shape[1])] = v
 
     blocks(rows, cols, first)
     greet_wait(tiles)
     source.start()
+    for fetch in fetches:
+        fetch.wait()
     fields, c0, c1 = w_in.shape[2], w_block.shape[3], w_coarse.shape[3]
-    heighten(k_in, w_in, (fields,))
+    heighten(k_in, w_in, 0, fields)
     widen(k_block, w_block, (c0,))
     k_mix[...] = jnp.zeros_like(k_mix)
     k_mix[pl.ds(0, c0), pl.ds(0, c0)] = w_mix[...]
@@ -346,7 +353,8 @@
     encoded.start()
     widen(k_down, w_down, (c0,))
     widen(k_coarse, w_coarse, (c1,))
-    heighten(k_decode, w_decode, (c1, c0))
+    heighten(k_wide, w_decode, 0, c1)
+    heighten(k_skip, w_decode, c1, c0)
     encoded.finish()
 
     def block(*at):
@@ -383,6 +391,11 @@
     blocks(c_rows, c_cols, coarse)
     two.start()
     skip.finish()
+
+    def decode_skip(*at):
+        put(partial, conv_block([skip.x], k_skip, cols, 1, *at), 0, cols, *at)
+
+    blocks(rows, cols, decode_skip)
     two.finish()
 
     for q in range(wide.shape[0]):
@@ -400,7 +413,8 @@
 
     def decode(*at):
         face, faces, row, height = at
-        v = jax.nn.gelu(conv_block([wide, skip.x], k_decode, cols, 1, *at)).astype(BF16)
+        total = get(partial, 0, cols, *at) + conv_block([wide], k_wide, cols, 1, *at)
+        v = jax.nn.gelu(total).astype(BF16)
         read = lax.dot_general(k_out[...], v, (((1,), (1,)), ((), ())), preferred_element_type=F32)
         for f in range(faces):
             for r in range(height):
@@ -418,7 +432,6 @@
     _, fields, rows, cols = state.shape
     tiles = lax.axis_size("tile")
     c0, c1 = weight_block.shape[2], weight_down.shape[2]
-    src = jnp.transpose(state, (0, 2, 3, 1))
     g0, g1 = groups_of(c0), groups_of(c1)
     plans = [
         (rows, cols, 1, 1),
@@ -430,6 +443,7 @@
     ]
     scratch = [s for plan in plans for s in Halo.shapes(*plan, tiles)]
     scratch.append(pltpu.VMEM((g1, 3, rows + 2, cols + 2 * EDGE, LANES), F32))
+    scratch.append(pltpu.VMEM((g0, 3, rows, cols + 2 * EDGE, LANES), F32))
     scratch += [
         pltpu.VMEM(s, BF16)
         for s in (
@@ -438,21 +452,24 @@
             (g0 * LANES, g0 * LANES),
             (3, g1 * LANES, 3 * g0 * LANES),
             (3, g1 * LANES, 3 * g1 * LANES),
-            (3, 3 * (g1 + g0) * LANES, g0 * LANES),
+            (3, 3 * g1 * LANES, g0 * LANES),
+            (3, 3 * g0 * LANES, g0 * LANES),
             (fields, g0 * LANES),
         )
     ]
     weights = [jnp.swapaxes(weight_in, 2, 3), weight_block, weight_mix, weight_down, weight_coarse,
                jnp.swapaxes(weight_decode, 2, 3), readout_matrix]
+    scratch += [pltpu.VMEM(v.shape, BF16) for v in weights]
+    scratch.append(pltpu.SemaphoreType.DMA((len(weights),)))
     advanced = pl.pallas_call(
         functools.partial(kernel, plans, tiles),
         out_shape=jax.ShapeDtypeStruct((3, fields, rows, cols), F32),
-        in_specs=[pl.BlockSpec(memory_space=pltpu.VMEM)] * 9,
+        in_specs=[pl.BlockSpec(memory_space=pltpu.VMEM)] + [pl.BlockSpec(memory_space=pl.ANY)] * 7,
         out_specs=pl.BlockSpec(memory_space=pltpu.VMEM),
         scratch_shapes=scratch,
         compiler_params=pltpu.CompilerParams(
             collective_id=0, has_side_effects=True, vmem_limit_bytes=60 * 1024 * 1024),
-    )(state, src, *weights)
+    )(state, *weights)
     return advanced[:, None]
 
 

time: 42 us -> 39.9 us (0.950)
  local copies, waits for them, and re-layouts: 3.47 us -> 1.62 us
    unnamed x2 -> x1, local copies, waits for them, and re-layouts: 3.47 us -> 1.62 us
where the time goes in v4:
time: 39.9 us; the launch traced here: 39.8 us
  Pallas kernels  38.1 us (95%)
  local copies, waits for them, and re-layouts  1.62 us (4%)
    pallas_call x1, Pallas kernels, shards(): pl.pallas_call(functools.partial(kernel, plans, tiles), out_shape=jax.Sha...  38.1 us
    unnamed x1, local copies, waits for them, and re-layouts  1.62 us

profile of v4, /device:TPU:0, one launch (start us, length us, event | category | flops | bytes accessed | tf_op | source)
XLA Modules:
  0.0 39.8 jit_solution(7602772348695176488)
XLA Ops:
  0.0 38.1 %shard_map.82 = f32[3,16,8,32]{3,2,1,0:T(8,128)} custom-call(f32[3,16,8,32]{3,2,1,0:T(8,128)} %bitcast.8, bf16[3,3,16,90]{3,2,1,0:T(8,128)(2,1)} %bitcast.9, bf16[3,3,90,90]{3,2,1,0:T(8,128)(2,1)} %refs_1_.1, bf16[90,90]{1,0:T(8,128)(2,1)} %refs_2_.1, bf16[3,3,180,90]{3,2,1,0:T(8,128)(2,1)} %refs_3_.1, bf16[3,3,180,180]{3,2,1,0:T(8,128)(2,1)} %refs_4_.1, ...), custom_call_target="tpu_custom_call" | custom-call | tf_op jit(solution)/shard_map/pallas_call | solution.py:464
  38.1 1.6 %copy.11 = f32[3,1,16,8,32]{4,3,2,1,0:T(8,128)} copy(f32[3,1,16,8,32]{4,3,2,1,0:T(8,128)} %bitcast.6) | data formatting | bytes 98304
